TPU v7x, 32 devices: a whole 2x2x4 slice. The times are simulated.
32 devices in a mesh: seq: 4 (over z), exp: 8 (over y, x, core).
Axes of the slice: x: 2, y: 2, z: 4, core: 2. Of those that a mesh axis runs over, the one named last changes fastest.
Arguments:
- hidden: bfloat16 [8, 1024, 768], P('exp', 'seq'), may hold values from -40 to 40
- ssm_input: bfloat16 [8, 1024, 1536], P('exp', 'seq'), may hold values from -6 to 6
- ssm_gate: bfloat16 [8, 1024, 1536], P('exp', 'seq'), may hold values from -6 to 6
- write_proj: bfloat16 [8, 1024, 128], P('exp', 'seq'), may hold values from -1 to 1
- read_proj: bfloat16 [8, 1024, 128], P('exp', 'seq'), may hold values from -1 to 1
- dt_raw: float32 [8, 24, 1024], P('exp', None, 'seq'), may hold values from -4.5 to 150
- dt_bias: float32 [24], replicated, may hold values from -2 to -0.5
- a_log: float32 [24], replicated, may hold values from -7 to -1.2
- d_skip: float32 [24], replicated, may hold values from 0.5 to 2
- norm_gain: float32 [1536], replicated, may hold values from 0.25 to 1.75
- out_weight: bfloat16 [1536, 768], replicated, may hold values from -0.15625 to 0.15625
- moe_gain: float32 [768], replicated, may hold values from 0.25 to 1.75
- expert_ids: int32 [8, 1024, 2], P('exp', 'seq'), may hold values from 0 to 7, all different within a row; in each aligned block of 256 rows (0 to 255, 256 to 511, ..., all dimensions but the last counted through in order) at most 96 rows name the same one
- gate_values: float32 [8, 1024, 2], P('exp', 'seq'), may hold values from 0.2 to 1
- w_gate: bfloat16 [8, 768, 1536], P('exp'), may hold values from -0.21875 to 0.21875
- w_up: bfloat16 [8, 768, 1536], P('exp'), may hold values from -0.21875 to 0.21875
- w_down: bfloat16 [8, 1536, 768], P('exp'), may hold values from -0.15625 to 0.15625
Outputs:
- layer_out: bfloat16 [8, 1024, 768], P('exp', 'seq')
Inputs may be any that keep to these rules, and one draw needn't show every extreme that they name: `expert_ids`: the two experts of a position differ. In each block of 256 positions of one trace (the rows of one device) no expert is named by more than 96 of the block's positions, a bound that some block reaches.
All inputs are finite; a program needn't handle non-finite values.
Results may differ from a plain program's by a relative error of at most 0.005.
Values may be sent and summed in bfloat16 or wider, within the bound.
No kernel may reach another device: no remote copies, remote signals or barrier semaphores. Data moves between devices by JAX's collectives and lax.ppermute only.
A program may use at most 64 MiB of HBM per device.

v0:
```python
import jax
import jax.numpy as jnp
from jax import lax
from jax.sharding import PartitionSpec as P

EPS = 1e-05


def prefix(value, axis, join, neutral):
    count, mine = (lax.axis_size(axis), lax.axis_index(axis))
    pieces = jax.tree.map(lambda part: lax.all_gather(part, axis), value)
    total = jax.tree.map(
        lambda part, zero: jnp.full_like(part, 0) + jnp.asarray(zero, part.dtype), value, neutral
    )

    def hop(position, total):
        longer = join(total, jax.tree.map(lambda part: part[position], pieces))
        return jax.tree.map(lambda new, old: jnp.where(position < mine, new, old), longer, total)

    return lax.fori_loop(0, count - 1, hop, total)


def local_block(signal, write_rows, read_rows, raw_steps, dt_bias, a_log):
    positions = signal.shape[0]
    head_count = raw_steps.shape[0]
    step_size = jax.nn.softplus(raw_steps + dt_bias[:, None])
    log_decay = -jnp.exp(a_log)[:, None] * step_size
    cumulative = jnp.cumsum(log_decay, axis=1)
    scores = jnp.einsum("tn,sn->ts", read_rows, write_rows, preferred_element_type=jnp.float32)
    causal = jnp.arange(positions)[:, None] >= jnp.arange(positions)[None, :]
    spread = cumulative[:, :, None] - cumulative[:, None, :]
    kernel = jnp.where(causal[None], jnp.exp(jnp.where(causal[None], spread, 0.0)), 0.0)
    weights = (scores[None] * kernel * step_size[:, None, :]).astype(jnp.bfloat16)
    signal_heads = signal.reshape(positions, head_count, -1)
    y_intra = jnp.einsum("hts,shp->thp", weights, signal_heads, preferred_element_type=jnp.float32)
    to_end = jnp.exp(cumulative[:, -1:] - cumulative) * step_size
    scaled = (signal_heads.astype(jnp.float32) * to_end.T[:, :, None]).astype(jnp.bfloat16)
    block_state = jnp.einsum("shp,sn->hpn", scaled, write_rows, preferred_element_type=jnp.float32)
    return (y_intra, block_state, jnp.exp(cumulative[:, -1]), cumulative)


def finish(y_intra, cumulative, read_rows, incoming, signal, gate_rows, d_skip, norm_gain):
    positions = signal.shape[0]
    signal_heads = signal.reshape(positions, d_skip.shape[0], -1).astype(jnp.float32)
    carried = jnp.einsum(
        "tn,hpn->thp", read_rows.astype(jnp.float32), incoming, precision=lax.Precision.HIGHEST
    )
    mixed = (
        y_intra + jnp.exp(cumulative).T[:, :, None] * carried + d_skip[None, :, None] * signal_heads
    )
    mixed = mixed.reshape(positions, -1) * jax.nn.silu(gate_rows.astype(jnp.float32))
    scale = lax.rsqrt(jnp.mean(mixed * mixed, axis=-1, keepdims=True) + EPS)
    return (mixed * scale * norm_gain).astype(jnp.bfloat16)


def slot_targets(expert_rows, experts, capacity):
    flat_ids = expert_rows.reshape(-1)
    hits = (flat_ids[:, None] == jnp.arange(experts, dtype=jnp.int32)[None, :]).astype(jnp.int32)
    before = jnp.cumsum(hits, axis=0) - hits
    slot = jnp.sum(before * hits, axis=1, dtype=jnp.int32).reshape(expert_rows.shape)
    return expert_rows * capacity + slot


def connect_blocks(earlier, later):
    return (earlier[0] * later[0], later[0][:, None, None] * earlier[1] + later[1])


def run_expert(received, gate_mat, up_mat, down_mat):
    sources, slot_count, width = received.shape
    flat_rows = received.reshape(-1, width)
    gate_portion = jnp.dot(flat_rows, gate_mat, preferred_element_type=jnp.float32)
    up_part = jnp.dot(flat_rows, up_mat, preferred_element_type=jnp.float32)
    active = (jax.nn.silu(gate_portion) * up_part).astype(jnp.bfloat16)
    result = jnp.dot(active, down_mat, preferred_element_type=jnp.float32).astype(jnp.bfloat16)
    return result.reshape(sources, slot_count, width)


def on_device(
    hidden,
    ssm_input,
    ssm_gate,
    write_proj,
    read_proj,
    dt_raw,
    dt_bias,
    a_log,
    d_skip,
    norm_gain,
    out_weight,
    moe_gain,
    expert_ids,
    gate_values,
    w_gate,
    w_up,
    w_down,
):
    signal = ssm_input[0]
    positions = signal.shape[0]
    y_intra, block_state, block_decay, cumulative = local_block(
        signal, write_proj[0], read_proj[0], dt_raw[0], dt_bias, a_log
    )
    identity = (jnp.ones_like(block_decay), jnp.zeros_like(block_state))
    _, incoming = prefix((block_decay, block_state), "seq", connect_blocks, identity)
    gated = finish(
        y_intra, cumulative, read_proj[0], incoming, signal, ssm_gate[0], d_skip, norm_gain
    )
    stream = hidden[0].astype(jnp.float32) + jnp.dot(
        gated, out_weight, preferred_element_type=jnp.float32
    )
    normed = (
        stream * lax.rsqrt(jnp.mean(stream * stream, axis=-1, keepdims=True) + EPS) * moe_gain
    ).astype(jnp.bfloat16)
    width = normed.shape[1]
    experts = lax.axis_size("exp") * w_gate.shape[0]
    capacity = max(2, 3 * positions // experts)
    targets = slot_targets(expert_ids[0], experts, capacity)
    owners = jnp.full((experts * capacity,), positions, jnp.int32)
    owners = owners.at[targets.reshape(-1)].set(
        jnp.repeat(jnp.arange(positions, dtype=jnp.int32), 2)
    )
    padded = jnp.concatenate([normed, jnp.zeros((1, width), jnp.bfloat16)], axis=0)
    buffer = jnp.take(padded, owners, axis=0)
    buffer = buffer.reshape(experts, capacity, width)
    computed = run_expert(
        lax.all_to_all(buffer, "exp", split_axis=0, concat_axis=0, tiled=True),
        w_gate[0],
        w_up[0],
        w_down[0],
    )
    returned = lax.all_to_all(computed, "exp", split_axis=0, concat_axis=0, tiled=True)
    back_rows = returned.reshape(experts * capacity, width)
    first = jnp.take(back_rows, targets[:, 0], axis=0).astype(jnp.float32)
    second = jnp.take(back_rows, targets[:, 1], axis=0).astype(jnp.float32)
    weights_here = gate_values[0]
    total = stream + weights_here[:, 0:1] * first + weights_here[:, 1:2] * second
    return total.astype(jnp.bfloat16)[None]


def solution(mesh):
    in_specs = (
        P("exp", "seq", None),
        P("exp", "seq", None),
        P("exp", "seq", None),
        P("exp", "seq", None),
        P("exp", "seq", None),
        P("exp", None, "seq"),
        P(),
        P(),
        P(),
        P(),
        P(),
        P(),
        P("exp", "seq", None),
        P("exp", "seq", None),
        P("exp", None, None),
        P("exp", None, None),
        P("exp", None, None),
    )
    out_specs = P("exp", "seq", None)
    return jax.shard_map(
        on_device, mesh=mesh, in_specs=in_specs, out_specs=out_specs, check_vma=False
    )
```

profile of v0, /device:TPU:0, one launch (start us, length us, event | category | flops | bytes accessed | tf_op | source)
XLA Modules:
  0.0 173.9 jit_solution(16051418273362553127)
XLA Ops:
  10.3 1.5 multiply_bitcast_fusion
  11.8 1.4 copy.44
  13.5 1.3 fusion.35
  17.3 13.5 %all-reduce.1 = f32[96]{0:T(128)S(1)} all-reduce(f32[96]{0:T(128)S(1)} %dynamic-update-slice), channel_id=2, replica_groups=mesh['seq'=4,'exp'=8] {'seq'}, use_global_device_ids=true, to_apply=%add.1 | all-reduce | flops 96 | bytes 768
  36.4 2.6 %scatter_custom_fusion = s32[768]{0:T(1024)S(1)} fusion(s32[512]{0:T(512)S(1)} %bitcast.139, s32[512]{0:T(512)} %reshape.249, s32[]{:T(128)} %constant.80.clone.1), kind=kCustom, calls=%fused_computation.85 | custom fusion | bytes 3584 | tf_op jit(solution)/shard_map/scatter | solution.py:118
  39.1 2.6 %copy.47 = f32[1,256,1536]{1,2,0:T(8,128)} copy(bf16[1,256,1536]{2,1,0:T(8,128)(2,1)} %param.23) | data formatting | bytes 2359296 | tf_op jit(solution)/shard_map/convert_element_type | solution.py:51
  42.5 38.7 %all-gather.4.cloned.1.call-done = f32[96,64,128]{2,1,0:T(8,128)} async-done(((f32[24,64,128]{2,1,0:T(8,128)}), f32[96,64,128]{2,1,0:T(8,128)}) %all-gather.4.cloned.1.call-update) | async-done | bytes 3145744 | tf_op jit(solution)/shard_map/all_gather | solution.py:11
  81.2 6.0 %while.14 = (s32[]{:T(128)}, f32[24,64,128]{2,1,0:T(8,128)S(1)}, s32[]{:T(128)}, f32[4,24]{1,0:T(4,128)}, f32[4,24,64,128]{3,2,1,0:T(8,128)}, /*index=5*/s32[]{:T(128)}, s32[]{:T(128)}) while((s32[]{:T(128)}, f32[24,64,128]{2,1,0:T(8,128)S(1)}, s32[]{:T(128)}, f32[4,24]{1,0:T(4,128)}, f32[4,24,64,128]{3,2,1,0:T(8,128)}, ...), condition=%wide.region_3.4_spmd.clone, body=%wide.region_2.3_spmd.clone.sunk | while | flops 786436 | bytes 2359697 | solution.py:20
  81.8 1.3 fusion.57
  83.8 1.3 fusion.57
  88.8 4.5 %multiply_reduce_fusion = (f32[256]{0:T(256)S(1)}, f32[256,24,64]{0,2,1:T(8,128)}) fusion(f32[256,24,64]{0,2,1:T(8,128)S(1)} %bitcast.131, bf16[256,24,64]{0,2,1:T(8,128)(2,1)S(1)} %bitcast.129, f32[24]{0:T(128)S(1)} %copy-done.17, f32[24,64,256]{2,1,0:T(8,128)S(1)} %fusion.33, f32[256,24]{0,1:T(8,128)} %get-tuple-element.135, ...), kind=kOutput, calls=%fused_computation.34 | convolution fusion | flops 215482112 | bytes 5907552 | tf_op jit(solution)/shard_map/hts,shp->thp/dot_general | solution.py:35
  93.4 3.1 %copy.46 = f32[256,1536]{1,0:T(8,128)} copy(f32[256,1536]{0,1:T(8,128)} %bitcast.132) | data formatting | bytes 3145728 | tf_op jit(solution)/shard_map/reshape | solution.py:51
  96.5 3.4 %multiply_reduce_fusion.1 = (f32[256]{0:T(256)S(1)}, f32[256,768]{1,0:T(8,128)S(1)}) fusion(bf16[1536,768]{1,0:T(8,128)(2,1)} %param.31, f32[256,1536]{1,0:T(8,128)} %copy.46, f32[1536]{0:T(1024)S(1)} %copy-done.16, f32[256]{0:T(256)S(1)} %add_rsqrt_fusion.1, bf16[1,256,1536]{2,1,0:T(8,128)(2,1)S(1)} %copy-done.6, bf16[1,256,768]{2,1,0:T(8,128)(2,1)} %param.21), kind=kOutput, calls=%fused_computation.41 | convolution fusion | flops 608304896 | bytes 5906432 | tf_op jit(solution)/shard_map/dot_general | solution.py:107
  101.0 3.5 %gather_fusion = bf16[768,768]{1,0:T(8,128)(2,1)} fusion(bf16[257,768]{1,0:T(8,128)(2,1)S(1)} %concatenate.3, s32[1024]{0:T(1024)S(1)} %pad_clamp_fusion.2), kind=kCustom, calls=%fused_computation.2 | custom fusion | bytes 2362368 | tf_op jit(solution)/shard_map/jit(_take)/gather | solution.py:122
  104.5 2.5 %broadcast_select_fusion = bf16[8,96,768]{2,1,0:T(8,128)(2,1)} fusion(bf16[8,96,768]{2,1,0:T(8,128)(2,1)} %bitcast.128, pred[8,96]{1,0:T(8,128)(4,1)S(1)} %broadcast_in_dim.78), kind=kLoop, calls=%fused_computation.38 | loop fusion | flops 589824 | bytes 2360064 | tf_op jit(solution)/shard_map/jit(_take)/select_n | solution.py:122
  106.9 3.9 %all-to-all-start = ((bf16[8,96,768]{2,1,0:T(8,128)(2,1)}), bf16[8,96,768]{2,1,0:T(8,128)(2,1)S(1)}, u32[]{:S(2)}, u32[]{:S(2)}) async-start(bf16[8,96,768]{2,1,0:T(8,128)(2,1)} %broadcast_select_fusion), calls=%async_computation | async-start | bytes 2359296 | tf_op jit(solution)/shard_map/all_to_all | solution.py:125
  111.6 15.9 %all-to-all-done = bf16[8,96,768]{2,1,0:T(8,128)(2,1)S(1)} async-done(((bf16[8,96,768]{2,1,0:T(8,128)(2,1)}), bf16[8,96,768]{2,1,0:T(8,128)(2,1)S(1)}, u32[]{:S(2)}, u32[]{:S(2)}) %all-to-all-start) | async-done | bytes 1179680 | tf_op jit(solution)/shard_map/all_to_all | solution.py:125
  127.6 4.1 %fusion.11 = f32[768,1536]{1,0:T(8,128)} fusion(bf16[768,768]{1,0:T(8,128)(2,1)S(1)} %bitcast.134, bf16[1,768,1536]{2,1,0:T(8,128)(2,1)S(1)} %copy-done), kind=kOutput, calls=%fused_computation.19 | convolution fusion | flops 1811939328 | bytes 8257536 | tf_op jit(solution)/shard_map/dot_general | solution.py:71
  131.7 8.8 %fusion.23 = bf16[768,768]{1,0:T(8,128)(2,1)} fusion(bf16[1,1536,768]{2,1,0:T(8,128)(2,1)} %param.37, f32[768,1536]{1,0:T(8,128)} %fusion.11, bf16[768,768]{1,0:T(8,128)(2,1)S(1)} %bitcast.135, bf16[1,768,1536]{2,1,0:T(8,128)(2,1)} %param.36), kind=kOutput, calls=%fused_computation.36 | convolution fusion | flops 3631546368 | bytes 11796480 | tf_op jit(solution)/shard_map/dot_general | solution.py:74
  140.5 3.6 %all-to-all-start.1 = ((bf16[8,96,768]{2,1,0:T(8,128)(2,1)}), bf16[8,96,768]{2,1,0:T(8,128)(2,1)S(1)}, u32[]{:S(2)}, u32[]{:S(2)}) async-start(bf16[8,96,768]{2,1,0:T(8,128)(2,1)} %bitcast.133), calls=%async_computation.1 | async-start | bytes 2359296 | tf_op jit(solution)/shard_map/all_to_all | solution.py:130
  146.7 14.2 %all-to-all-done.1 = bf16[8,96,768]{2,1,0:T(8,128)(2,1)S(1)} async-done(((bf16[8,96,768]{2,1,0:T(8,128)(2,1)}), bf16[8,96,768]{2,1,0:T(8,128)(2,1)S(1)}, u32[]{:S(2)}, u32[]{:S(2)}) %all-to-all-start.1) | async-done | bytes 1179680 | tf_op jit(solution)/shard_map/all_to_all | solution.py:130
  160.8 1.9 %gather_fusion.2 = bf16[256,768]{1,0:T(8,128)(2,1)} fusion(bf16[768,768]{1,0:T(8,128)(2,1)S(1)} %bitcast.125, s32[1024]{0:T(1024)S(1)} %pad_clamp_fusion), kind=kCustom, calls=%fused_computation.1.clone | custom fusion | bytes 787456 | tf_op jit(solution)/shard_map/jit(_take)/gather | solution.py:133
  162.8 1.9 %gather_fusion.1 = bf16[256,768]{1,0:T(8,128)(2,1)} fusion(bf16[768,768]{1,0:T(8,128)(2,1)S(1)} %bitcast.126, s32[1024]{0:T(1024)S(1)} %pad_clamp_fusion.1), kind=kCustom, calls=%fused_computation.clone | custom fusion | bytes 787456 | tf_op jit(solution)/shard_map/jit(_take)/gather | solution.py:132
  164.7 2.4 %fusion.31 = bf16[1,256,768]{2,1,0:T(8,128)(2,1)} fusion(f32[256,768]{1,0:T(8,128)} %copy-done.4, bf16[256,768]{1,0:T(8,128)(2,1)} %gather_fusion.2, bf16[256,768]{1,0:T(8,128)(2,1)} %gather_fusion.1, f32[256]{0:T(256)S(1)} %bitcast.138, f32[256]{0:T(256)S(1)} %bitcast.137, pred[256]{0:T(512)(128)(4,1)S(1)} %copy-done.15, pred[256]{0:T(512)(128)(4,1)} %get-tuple-element.145), kind=kLoop, calls=%fused_computation.44 | loop fusion | flops 1769472 | bytes 1968640 | tf_op jit(solution)/shard_map/broadcast_in_dim | solution.py:136
  (92 shorter events, 21.6 us)
Async XLA Ops:
  6.5 121.0 %copy-start = (bf16[1,768,1536]{2,1,0:T(8,128)(2,1)S(1)}, bf16[1,768,1536]{2,1,0:T(8,128)(2,1)}, u32[]{:S(2)}) copy-start(bf16[1,768,1536]{2,1,0:T(8,128)(2,1)} %param.35) | copy-start | bytes 7077892
  6.5 74.6 %all-gather.4.cloned.1.call-start = ((), (), s32[]{:S(2)}) async-start(), calls=%async_computation.2 | async-start | bytes 3932160 | tf_op jit(solution)/shard_map/all_gather | solution.py:11
  9.7 0.6 copy-start.10
  11.8 1.6 copy-start.7
  13.2 1.5 copy-start.2
  13.4 1.4 copy-start.14
  13.4 2.3 %copy-start.18 = (u32[32]{0:T(128)S(1)}, u32[32]{0:T(128)}, u32[]{:S(2)}) copy-start(u32[32]{0:T(128)} %constant.102) | copy-start | bytes 388
  14.9 26.7 %copy-start.1 = (s32[1,256,2]{2,1,0:T(8,128)}, s32[1,256,2]{2,1,0:T(8,128)S(1)}, u32[]{:S(2)}) copy-start(s32[1,256,2]{2,1,0:T(8,128)S(1)} %copy.48) | copy-start | bytes 6148
  33.4 8.9 %copy-start.8 = (bf16[1,256,128]{2,1,0:T(8,128)(2,1)S(1)}, bf16[1,256,128]{2,1,0:T(8,128)(2,1)}, u32[]{:S(2)}) copy-start(bf16[1,256,128]{2,1,0:T(8,128)(2,1)} %param.25) | copy-start | bytes 196612
  35.7 0.7 copy-start.11
  87.2 1.1 copy-start.3
  87.2 1.6 copy-start.5
  87.2 1.6 copy-start.9
  87.2 1.6 copy-start.17
  93.3 3.1 %copy-start.6 = (bf16[1,256,1536]{2,1,0:T(8,128)(2,1)S(1)}, bf16[1,256,1536]{2,1,0:T(8,128)(2,1)}, u32[]{:S(2)}) copy-start(bf16[1,256,1536]{2,1,0:T(8,128)(2,1)} %param.23) | copy-start | bytes 2359300
  93.4 3.1 %copy-start.16 = (f32[1536]{0:T(1024)S(1)}, f32[1536]{0:T(1024)}, u32[]{:S(2)}) copy-start(f32[1536]{0:T(1024)} %param.30) | copy-start | bytes 18436
  96.5 4.3 %copy-start.13 = (f32[768]{0:T(1024)S(1)}, f32[768]{0:T(1024)}, u32[]{:S(2)}) copy-start(f32[768]{0:T(1024)} %param.32) | copy-start | bytes 9220
  99.9 0.9 copy-start.4
  106.9 3.9 %copy-start.12 = (s32[512]{0:T(512)S(1)}, s32[512]{0:T(512)}, u32[]{:S(2)}) copy-start(s32[512]{0:T(512)} %copy-done.11) | copy-start | bytes 6148
  106.9 20.6 %all-to-all-start = ((bf16[8,96,768]{2,1,0:T(8,128)(2,1)}), bf16[8,96,768]{2,1,0:T(8,128)(2,1)S(1)}, u32[]{:S(2)}, u32[]{:S(2)}) async-start(bf16[8,96,768]{2,1,0:T(8,128)(2,1)} %broadcast_select_fusion), calls=%async_computation | async-start | bytes 2359296 | tf_op jit(solution)/shard_map/all_to_all | solution.py:125
  140.5 20.3 %all-to-all-start.1 = ((bf16[8,96,768]{2,1,0:T(8,128)(2,1)}), bf16[8,96,768]{2,1,0:T(8,128)(2,1)S(1)}, u32[]{:S(2)}, u32[]{:S(2)}) async-start(bf16[8,96,768]{2,1,0:T(8,128)(2,1)} %bitcast.133), calls=%async_computation.1 | async-start | bytes 2359296 | tf_op jit(solution)/shard_map/all_to_all | solution.py:130
  162.8 1.9 %copy-start.15 = (pred[256]{0:T(512)(128)(4,1)S(1)}, pred[256]{0:T(512)(128)(4,1)}, u32[]{:S(2)}) copy-start(pred[256]{0:T(512)(128)(4,1)} %get-tuple-element.144) | copy-start | bytes 772
Sparse Core Ops, SparseCore 0:
  14.9 66.2 all-gather.3
where the time goes:
time: 175 us; the launch traced here: 174 us
  waiting for transfers between devices  68.8 us (39%)
  local copies, waits for them, and re-layouts  28.9 us (17%)
  matrix products  23.2 us (13%)
  other arithmetic  17.7 us (10%)
  between operations  14.3 us (8%)
  blocking collectives  13.5 us (8%)
  starting transfers between devices  7.44 us (4%)
    all_gather x1, waiting for transfers between devices, prefix(): pieces = jax.tree.map(lambda part: lax.all_gather(part, axis), value)  38.7 us
    all_to_all x1, waiting for transfers between devices, on_device(): lax.all_to_all(buffer, 'exp', split_axis=0, concat_axis=0, tiled=True)  15.9 us
    all_to_all x1, waiting for transfers between devices, on_device(): lax.all_to_all(computed, 'exp', split_axis=0, concat_axis=0, tiled=True)  14.2 us
    unnamed x1, blocking collectives  13.5 us
    dot_general x1, matrix products, run_expert(): jnp.dot(active, down_mat, preferred_element_type=jnp.float32)  8.83 us
    unnamed x43, local copies, waits for them, and re-layouts  4.57 us
    dot_general x1, matrix products, local_block(): jnp.einsum('hts,shp->thp', weights, signal_heads, preferred_element_type=...  4.52 us
    dot_general x1, matrix products, run_expert(): jnp.dot(flat_rows, gate_mat, preferred_element_type=jnp.float32)  4.11 us
  transfers between devices with their start and end apart: 3, of which 3 were waited for; matrix products, arithmetic and copies ran while one was open for 10% of the time, Pallas kernels for 0%

commit v1 on v0

v1 whole, which is shorter than its diff:
```python
import functools

import jax
import jax.numpy as jnp
from jax import lax
from jax.experimental import pallas as pl
from jax.experimental.pallas import tpu as pltpu
from jax.sharding import PartitionSpec as P

EPS = 1e-05
F32 = jnp.float32
BF16 = jnp.bfloat16
CHUNKS = 3


def call(body, name, out_shape, flops, nbytes, **kwargs):
    return pl.pallas_call(
        body,
        out_shape=out_shape,
        name=name,
        compiler_params=pltpu.CompilerParams(vmem_limit_bytes=32 * 2**20),
        cost_estimate=pl.CostEstimate(flops=flops, bytes_accessed=nbytes, transcendentals=0),
        **kwargs,
    )


def dot(a, b):
    return jnp.dot(a, b, preferred_element_type=F32)


def dot_rows(a, b):
    return lax.dot_general(a, b, (((0,), (0,)), ((), ())), preferred_element_type=F32)


def pieces(value, count):
    parts = []
    for _ in range(count):
        part = value.astype(BF16)
        parts.append(part)
        value = value - part.astype(F32)
    return parts


def iota(shape, dim):
    return lax.broadcasted_iota(jnp.int32, shape, dim)


def state_kernel(dt_ref, bias_ref, alog_ref, x_ref, write_ref, cum_ref, step_ref, decay_ref, *state_refs):
    length, inner = x_ref.shape
    heads = dt_ref.shape[0]
    raw = dt_ref[...].T + bias_ref[...]
    step = jnp.maximum(raw, 0.0) + jnp.log1p(jnp.exp(-jnp.abs(raw)))
    log_decay = -jnp.exp(alog_ref[...]) * step
    lower = (iota((length, length), 0) >= iota((length, length), 1)).astype(F32).astype(BF16)
    cum = sum(dot(lower, part) for part in pieces(log_decay, 3))
    last = cum[length - 1 : length, :]
    to_end = jnp.exp(jnp.minimum(last - cum, 0.0)) * step
    expand = (iota((heads, inner), 1) // (inner // heads) == iota((heads, inner), 0)).astype(F32).astype(BF16)
    decay = sum(dot(part, expand) for part in pieces(jnp.broadcast_to(jnp.exp(last), (8, heads)), 3))
    cum_ref[...] = cum
    step_ref[...] = step
    decay_ref[...] = decay[0:1, :]
    ends = pieces(to_end, 2)
    width = inner // len(state_refs)
    for k, state_ref in enumerate(state_refs):
        cols = slice(k * width, (k + 1) * width)
        wide = sum(dot(part, expand[:, cols]) for part in ends)
        scaled = (x_ref[:, cols].astype(F32) * wide).astype(BF16)
        state_ref[...] = dot_rows(write_ref[...], scaled).astype(BF16)


def intra_kernel(xor, capacity, cum_ref, step_ref, x_ref, gate_ref, write_ref, read_ref, skip_ref, ids_ref,
                 own_ref, factor_ref, route_ref, target_ref):
    length, inner = x_ref.shape
    heads = cum_ref.shape[1]
    half = length // 2
    cum = cum_ref[...]
    cum_rows = cum.T
    step_rows = step_ref[...].T
    scores = lax.dot_general(
        read_ref[...], write_ref[...], (((1,), (1,)), ((), ())), preferred_element_type=F32
    )
    scores = jnp.where(iota((length, length), 0) >= iota((length, length), 1), scores, 0.0)
    lanes = 2 * (inner // heads)
    first = iota((length, lanes), 1) < lanes // 2
    first_row = iota((1, lanes), 1) < lanes // 2
    for pair in range(heads // 2):
        cols = slice(pair * lanes, (pair + 1) * lanes)
        x = x_ref[:, cols]
        wide = x.astype(F32)
        masked = [jnp.where(first, wide, 0.0).astype(BF16), jnp.where(first, 0.0, wide).astype(BF16)]
        tops, bottoms = [], []
        for h in (2 * pair, 2 * pair + 1):
            here = cum[:, h : h + 1]
            there = cum_rows[h : h + 1, :]
            steps = step_rows[h : h + 1, :]
            top = jnp.exp(jnp.minimum(here[:half] - there[:, :half], 0.0))
            tops.append((scores[:half, :half] * top * steps[:, :half]).astype(BF16))
            bottom = jnp.exp(jnp.minimum(here[half:] - there, 0.0))
            bottoms.append((scores[half:, :] * bottom * steps).astype(BF16))
        y_top = dot(jnp.concatenate(tops, 1), jnp.concatenate([m[:half] for m in masked], 0))
        y_bottom = dot(jnp.concatenate(bottoms, 1), jnp.concatenate(masked, 0))
        y = jnp.concatenate([y_top, y_bottom], 0)
        skip = jnp.where(first_row, skip_ref[:, 2 * pair : 2 * pair + 1], skip_ref[:, 2 * pair + 1 : 2 * pair + 2])
        gate = gate_ref[:, cols].astype(F32)
        gate = gate / (1.0 + jnp.exp(-gate))
        grown = jnp.exp(jnp.where(first, cum[:, 2 * pair : 2 * pair + 1], cum[:, 2 * pair + 1 : 2 * pair + 2]))
        own_ref[:, cols] = (y + skip * wide) * gate
        factor_ref[:, cols] = grown * gate
    ids = ids_ref[...]
    lane = iota((length, 128), 1)
    hits = [(ids[:, k : k + 1] == lane).astype(F32) for k in range(2)]
    earlier = (iota((length, length), 0) > iota((length, length), 1)).astype(F32).astype(BF16)
    before = dot(earlier, (hits[0] + hits[1]).astype(BF16))
    if xor:
        ids = ids ^ lax.axis_index("exp")
    slots = route_ref.shape[0]
    rows = jnp.zeros((length, slots), F32)
    for k in range(2):
        slot = jnp.sum(before * hits[k], axis=1, keepdims=True).astype(jnp.int32)
        target = ids[:, k : k + 1] * capacity + slot
        target_ref[:, k : k + 1] = target
        rows = jnp.where(target == iota((length, slots), 1), 1.0, rows)
    route_ref[...] = rows.T.astype(BF16)


def mix_kernel(chunks, *refs):
    earlier, latest = refs[:chunks], refs[chunks : 2 * chunks]
    (read_ref, own_ref, factor_ref, norm_ref, weight_ref, hidden_ref, gain_ref, route_ref) = refs[2 * chunks : 2 * chunks + 8]
    stream_ref, *buffer_refs, mixed_ref = refs[2 * chunks + 8 :]
    inner = own_ref.shape[1]
    width = inner // chunks
    total = 0.0
    for k in range(chunks):
        cols = slice(k * width, (k + 1) * width)
        incoming = (earlier[k][...].astype(F32) + latest[k][...].astype(F32)).astype(BF16)
        value = own_ref[:, cols] + factor_ref[:, cols] * dot(read_ref[...], incoming)
        mixed_ref[:, cols] = value
        total = total + jnp.sum(value * value, axis=1, keepdims=True)
    scale = lax.rsqrt(total / inner + EPS)
    gated = (mixed_ref[...] * scale * norm_ref[...]).astype(BF16)
    stream = hidden_ref[...].astype(F32) + dot(gated, weight_ref[...])
    stream_ref[...] = stream
    scale = lax.rsqrt(jnp.mean(stream * stream, axis=1, keepdims=True) + EPS)
    normed = (stream * scale * gain_ref[...]).astype(BF16)
    at = 0
    for buffer_ref in buffer_refs:
        rows = buffer_ref.shape[0]
        buffer_ref[...] = dot(route_ref[at : at + rows, :], normed).astype(BF16)
        at += rows


def expert_kernel(count, *refs):
    rows, (gate_ref, up_ref, down_ref) = refs[:count], refs[count : count + 3]
    outs, total = refs[count + 3 : 2 * count + 3], refs[2 * count + 3]
    x = jnp.concatenate([r[...] for r in rows], 0)
    gate = dot(x, gate_ref[...])
    active = (gate / (1.0 + jnp.exp(-gate)) * dot(x, up_ref[...])).astype(BF16)
    part = dot(active, down_ref[...])
    step, last = pl.program_id(0), pl.num_programs(0) - 1

    @pl.when(step == 0)
    def _():
        total[...] = part

    @pl.when(step > 0)
    def _():
        total[...] += part

    @pl.when(step == last)
    def _():
        at = 0
        for out in outs:
            out[...] = total[at : at + out.shape[0], :].astype(BF16)
            at += out.shape[0]


def run_expert(rows, w_gate, w_up, w_down):
    count, (width, hidden) = len(rows), w_gate.shape
    tile = hidden // 3
    sizes = [r.shape[0] for r in rows]
    row_specs = [pl.BlockSpec((n, width), lambda j: (0, 0)) for n in sizes]
    return call(
        functools.partial(expert_kernel, count),
        "experts",
        [jax.ShapeDtypeStruct((n, width), BF16) for n in sizes],
        6 * sum(sizes) * width * hidden,
        6 * width * hidden + 4 * sum(sizes) * width,
        grid=(hidden // tile,),
        in_specs=row_specs
        + [pl.BlockSpec((width, tile), lambda j: (0, j))] * 2
        + [pl.BlockSpec((tile, width), lambda j: (j, 0))],
        out_specs=row_specs,
        scratch_shapes=[pltpu.VMEM((sum(sizes), width), F32)],
    )(*rows, w_gate, w_up, w_down)


def combine_kernel(count, *refs):
    rows, (target_ref, values_ref, stream_ref, out_ref) = refs[:count], refs[count:]
    returned = jnp.concatenate([r[...] for r in rows], 0)
    total = stream_ref[...]
    for k in range(2):
        pick = (target_ref[:, k : k + 1] == iota((total.shape[0], returned.shape[0]), 1)).astype(F32).astype(BF16)
        total = total + values_ref[:, k : k + 1] * dot(pick, returned)
    out_ref[...] = total.astype(BF16)


def pinned(first, *later):
    return lax.optimization_barrier((first, *later))[1:]


def on_device(
    hidden,
    ssm_input,
    ssm_gate,
    write_proj,
    read_proj,
    dt_raw,
    dt_bias,
    a_log,
    d_skip,
    norm_gain,
    out_weight,
    moe_gain,
    expert_ids,
    gate_values,
    w_gate,
    w_up,
    w_down,
):
    signal, gate, write, read = ssm_input[0], ssm_gate[0], write_proj[0], read_proj[0]
    length, inner = signal.shape
    width = hidden.shape[2]
    heads, state = dt_raw.shape[1], write.shape[1]
    n_seq, n_exp = lax.axis_size("seq"), lax.axis_size("exp")
    experts = n_exp * w_gate.shape[0]
    capacity = max(2, 3 * length // experts)
    slots = experts * capacity
    direct = n_exp == 8 and capacity % 16 == 0 and w_gate.shape[0] == 1
    shape = jax.ShapeDtypeStruct

    cum, step, decay, *states = call(
        state_kernel,
        "block_state",
        [shape((length, heads), F32), shape((length, heads), F32), shape((1, inner), F32)]
        + [shape((state, inner // CHUNKS), BF16)] * CHUNKS,
        2 * length * state * inner,
        2 * length * inner,
    )(dt_raw[0], dt_bias[None], a_log[None], signal, write)

    part = inner // CHUNKS
    incoming = [jnp.zeros_like(s) for s in states]
    received = [lax.ppermute(s, "seq", [(0, 1)]) for s in states]
    for hop in range(2, n_seq):
        for k in range(CHUNKS):
            incoming[k] = incoming[k] + received[k]
            sent = decay[:, k * part : (k + 1) * part] * incoming[k].astype(F32) + states[k].astype(F32)
            sent = lax.optimization_barrier(sent.astype(BF16))
            received[k] = lax.ppermute(sent, "seq", [(hop - 1, hop)])

    own, factor, route, targets = call(
        functools.partial(intra_kernel, direct, capacity),
        "intra_block",
        [
            shape((length, inner), F32),
            shape((length, inner), F32),
            shape((slots, length), BF16),
            shape((length, 2), jnp.int32),
        ],
        4 * length * length * inner,
        12 * length * inner,
    )(cum, step, signal, gate, write, read, d_skip[None], expert_ids[0])

    blocks = [capacity] * n_exp if direct else [slots]
    stream, *buffers = call(
        functools.partial(mix_kernel, CHUNKS),
        "mix",
        [shape((length, width), F32)] + [shape((n, width), BF16) for n in blocks],
        2 * length * inner * width,
        8 * length * inner,
        scratch_shapes=[pltpu.VMEM((length, inner), F32)],
    )(
        *incoming,
        *received,
        read,
        own,
        factor,
        norm_gain[None],
        out_weight,
        hidden[0],
        moe_gain[None],
        route,
    )

    weights = (w_gate[0], w_up[0], w_down[0])
    if direct:
        swap = lambda rows, k: lax.ppermute(rows, "exp", [(i, i ^ k) for i in range(n_exp)])
        arrived, returned = [None] * n_exp, [None] * n_exp
        arrived[0] = buffers[0]
        for k in (6, 7, 4, 5, 2, 3, 1):
            arrived[k] = swap(buffers[k], k)
        for group in ((6, 7), (4, 5), (2, 3), (0, 1)):
            results = run_expert([arrived[k] for k in group], *weights)
            for k, rows in zip(group, results):
                returned[k] = rows if k == 0 else swap(rows, k)
    else:
        trade = lambda rows: lax.all_to_all(
            rows.reshape(n_exp, -1, width), "exp", split_axis=0, concat_axis=0, tiled=True
        ).reshape(-1, width)
        returned = [trade(run_expert([trade(buffers[0])], *weights)[0])]

    total = call(
        functools.partial(combine_kernel, len(returned)),
        "combine",
        shape((length, width), BF16),
        4 * length * slots * width,
        2 * slots * width,
    )(*returned, targets, gate_values[0], stream)
    return total[None]


def solution(mesh):
    in_specs = (
        P("exp", "seq", None),
        P("exp", "seq", None),
        P("exp", "seq", None),
        P("exp", "seq", None),
        P("exp", "seq", None),
        P("exp", None, "seq"),
        P(),
        P(),
        P(),
        P(),
        P(),
        P(),
        P("exp", "seq", None),
        P("exp", "seq", None),
        P("exp", None, None),
        P("exp", None, None),
        P("exp", None, None),
    )
    out_specs = P("exp", "seq", None)
    return jax.shard_map(
        on_device, mesh=mesh, in_specs=in_specs, out_specs=out_specs, check_vma=False
    )
```

time: 175 us -> 78.7 us (0.45)
  the two profiles are of different devices: /device:TPU:0 before, /device:TPU:17 now
where the time goes in v1:
time: 78.7 us; the launch traced here: 78.1 us
  starting transfers between devices  32.6 us (41%)
  Pallas kernels  20.7 us (26%)
  local copies, waits for them, and re-layouts  11.2 us (14%)
  waiting for transfers between devices  11 us (14%)
  other arithmetic  2.29 us (3%)
    ppermute x14, starting transfers between devices, on_device(): lax.ppermute(rows, 'exp', [(i, i ^ k) for i in range(n_exp)])  20.7 us
    pallas_call x4, Pallas kernels, run_expert(): call(functools.partial(expert_kernel, count), 'experts', [jax.ShapeDtypeS...  11.3 us
    unnamed x52, local copies, waits for them, and re-layouts  11.2 us
    ppermute x6, starting transfers between devices, on_device(): received[k] = lax.ppermute(sent, 'seq', [(hop - 1, hop)])  9.85 us
    ppermute x6, waiting for transfers between devices, on_device(): received[k] = lax.ppermute(sent, 'seq', [(hop - 1, hop)])  5.7 us
    ppermute x14, waiting for transfers between devices, on_device(): lax.ppermute(rows, 'exp', [(i, i ^ k) for i in range(n_exp)])  5.27 us
    pallas_call x1, Pallas kernels, on_device(): call(functools.partial(mix_kernel, CHUNKS), 'mix', [shape((length, width)...  3.45 us
    pallas_call x1, Pallas kernels, on_device(): call(functools.partial(intra_kernel, direct, capacity), 'intra_block', [s...  2.84 us
  transfers between devices with their start and end apart: 23, of which 4 were waited for; matrix products, arithmetic and copies ran while one was open for 5% of the time, Pallas kernels for 18%

profile of v1, /device:TPU:17, one launch (start us, length us, event | category | flops | bytes accessed | tf_op | source)
XLA Modules:
  0.0 78.1 jit_solution(4191895526007169629)
XLA Ops:
  4.1 1.5 %block_state.1 = (f32[256,24]{1,0:T(8,128)S(1)}, f32[256,24]{1,0:T(8,128)S(1)}, f32[1,1536]{1,0:T(1,128)S(1)}, bf16[128,512]{1,0:T(8,128)(2,1)S(1)}, bf16[128,51...) custom-call(f32[24,256]{1,0:T(8,128)S(1)} %bitcast.40, f32[1,24]{1,0:T(1,128)S(1)} %bitcast.42, f32[1,24]{1,0:T(1,128)S(1)} %bitcast.43, ...), custom_call_target="tpu_custom_call" | custom-call | flops 100663296 | bytes 786432 | tf_op jit(solution)/shard_map/block_state/pallas_call | solution.py:242
  7.7 1.3 %collective-permute-start.5 = (bf16[128,512]{1,0:T(8,128)(2,1)S(1)}, bf16[128,512]{1,0:T(8,128)(2,1)S(1)}, u32[]{:S(2)}, u32[]{:S(2)}) collective-permute-start(bf16[128,512]{1,0:T(8,128)(2,1)S(1)} %fusion.4), channel_id=1, source_target_pairs={{8,16},{9,17},{10,18},{11,19},{12,20},{13,21},{14,22},{15,23}} | collective-permute-start | bytes 393224 | tf_op jit(solution)/shard_map/ppermute | solution.py:259
  9.1 1.4 %collective-permute-start.3 = (bf16[128,512]{1,0:T(8,128)(2,1)S(1)}, bf16[128,512]{1,0:T(8,128)(2,1)S(1)}, u32[]{:S(2)}, u32[]{:S(2)}) collective-permute-start(bf16[128,512]{1,0:T(8,128)(2,1)S(1)} %fusion.2), channel_id=1, source_target_pairs={{8,16},{9,17},{10,18},{11,19},{12,20},{13,21},{14,22},{15,23}} | collective-permute-start | bytes 393224 | tf_op jit(solution)/shard_map/ppermute | solution.py:259
  10.6 1.3 %collective-permute-start.1 = (bf16[128,512]{1,0:T(8,128)(2,1)S(1)}, bf16[128,512]{1,0:T(8,128)(2,1)S(1)}, u32[]{:S(2)}, u32[]{:S(2)}) collective-permute-start(bf16[128,512]{1,0:T(8,128)(2,1)S(1)} %fusion), channel_id=1, source_target_pairs={{8,16},{9,17},{10,18},{11,19},{12,20},{13,21},{14,22},{15,23}} | collective-permute-start | bytes 393224 | tf_op jit(solution)/shard_map/ppermute | solution.py:259
  11.9 3.8 %collective-permute-done.5 = bf16[128,512]{1,0:T(8,128)(2,1)S(1)} collective-permute-done((bf16[128,512]{1,0:T(8,128)(2,1)S(1)}, bf16[128,512]{1,0:T(8,128)(2,1)S(1)}, u32[]{:S(2)}, u32[]{:S(2)}) %collective-permute-start.5) | collective-permute-done | bytes 131104 | tf_op jit(solution)/shard_map/ppermute | solution.py:259
  16.4 1.9 %collective-permute-start.8 = (bf16[128,512]{1,0:T(8,128)(2,1)}, bf16[128,512]{1,0:T(8,128)(2,1)}, u32[]{:S(2)}, u32[]{:S(2)}) collective-permute-start(bf16[128,512]{1,0:T(8,128)(2,1)} %get-tuple-element.59), channel_id=1, source_target_pairs={{16,24},{17,25},{18,26},{19,27},{20,28},{21,29},{22,30},{23,31}} | collective-permute-start | bytes 393224 | tf_op jit(solution)/shard_map/ppermute | solution.py:259
  18.4 1.8 %collective-permute-done.3 = bf16[128,512]{1,0:T(8,128)(2,1)S(1)} collective-permute-done((bf16[128,512]{1,0:T(8,128)(2,1)S(1)}, bf16[128,512]{1,0:T(8,128)(2,1)S(1)}, u32[]{:S(2)}, u32[]{:S(2)}) %collective-permute-start.3) | collective-permute-done | bytes 131104 | tf_op jit(solution)/shard_map/ppermute | solution.py:259
  20.9 2.0 %collective-permute-start.7 = (bf16[128,512]{1,0:T(8,128)(2,1)}, bf16[128,512]{1,0:T(8,128)(2,1)}, u32[]{:S(2)}, u32[]{:S(2)}) collective-permute-start(bf16[128,512]{1,0:T(8,128)(2,1)} %get-tuple-element.61), channel_id=1, source_target_pairs={{16,24},{17,25},{18,26},{19,27},{20,28},{21,29},{22,30},{23,31}} | collective-permute-start | bytes 393224 | tf_op jit(solution)/shard_map/ppermute | solution.py:259
  23.6 1.9 %collective-permute-start.6 = (bf16[128,512]{1,0:T(8,128)(2,1)}, bf16[128,512]{1,0:T(8,128)(2,1)}, u32[]{:S(2)}, u32[]{:S(2)}) collective-permute-start(bf16[128,512]{1,0:T(8,128)(2,1)} %get-tuple-element.63), channel_id=1, source_target_pairs={{16,24},{17,25},{18,26},{19,27},{20,28},{21,29},{22,30},{23,31}} | collective-permute-start | bytes 393224 | tf_op jit(solution)/shard_map/ppermute | solution.py:259
  25.6 1.5 %copy.18 = s32[1,256,2]{2,1,0:T(8,128)} copy(s32[1,256,2]{1,2,0:T(2,128)} %param.29) | data formatting | bytes 4096 | tf_op args[12]
  32.6 2.8 %intra_block.1 = (f32[256,1536]{1,0:T(8,128)S(1)}, f32[256,1536]{1,0:T(8,128)S(1)}, bf16[768,256]{1,0:T(8,128)(2,1)S(1)}, s32[256,2]{1,0:T(8,128)S(1)}) custom-call(f32[256,24]{1,0:T(8,128)S(1)} %copy-done.15, f32[256,24]{1,0:T(8,128)S(1)} %copy-done.17, bf16[256,1536]{1,0:T(8,128)(2,1)S(1)} %bitcast.31, bf16[256,1536]{1,0:T(8,128)(2,1)S(1)} %bitcast.32, ...), custom_call_target="tpu_custom_call" | custom-call | flops 402653184 | bytes 4718592 | tf_op jit(solution)/shard_map/intra_block/pallas_call | solution.py:261
  35.6 3.5 %mix.1 = (f32[256,768]{1,0:T(8,128)S(1)}, bf16[96,768]{1,0:T(8,128)(2,1)S(1)}, bf16[96,768]{1,0:T(8,128)(2,1)S(1)}, bf16[96,768]{1,0:T(8,128)(2,1)S(1)}, bf16[96...) custom-call(bf16[128,512]{1,0:T(8,128)(2,1)S(1)} %get-tuple-element., ...), custom_call_target="tpu_custom_call" | custom-call | flops 603979776 | bytes 3145728 | tf_op jit(solution)/shard_map/mix/pallas_call | solution.py:275
  39.0 2.2 %collective-permute-start.19 = (bf16[96,768]{1,0:T(8,128)(2,1)S(1)}, bf16[96,768]{1,0:T(8,128)(2,1)S(1)}, u32[]{:S(2)}, u32[]{:S(2)}) collective-permute-start(bf16[96,768]{1,0:T(8,128)(2,1)S(1)} %get-tuple-element.53), channel_id=1, source_target_pairs={{0,6},{1,7},{2,4},{3,5},{4,2},{5,3},{6,0},{7,1},{8,14},{9,15},{10,... | collective-permute-start | bytes 442376 | tf_op jit(solution)/shard_map/ppermute | solution.py:297
  41.3 3.6 %collective-permute-start.20 = (bf16[96,768]{1,0:T(8,128)(2,1)S(1)}, bf16[96,768]{1,0:T(8,128)(2,1)S(1)}, u32[]{:S(2)}, u32[]{:S(2)}) collective-permute-start(bf16[96,768]{1,0:T(8,128)(2,1)S(1)} %get-tuple-element.54), channel_id=1, source_target_pairs={{0,7},{1,6},{2,5},{3,4},{4,3},{5,2},{6,1},{7,0},{8,15},{9,14},{10,... | collective-permute-start | bytes 442376 | tf_op jit(solution)/shard_map/ppermute | solution.py:297
  47.3 2.9 %collective-permute-start.12 = (bf16[96,768]{1,0:T(8,128)(2,1)S(1)}, bf16[96,768]{1,0:T(8,128)(2,1)S(1)}, u32[]{:S(2)}, u32[]{:S(2)}) collective-permute-start(bf16[96,768]{1,0:T(8,128)(2,1)S(1)} %get-tuple-element.46), channel_id=1, source_target_pairs={{0,3},{1,2},{2,1},{3,0},{4,7},{5,6},{6,5},{7,4},{8,11},{9,10},{10,... | collective-permute-start | bytes 442376 | tf_op jit(solution)/shard_map/ppermute | solution.py:297
  50.9 1.4 %collective-permute-start.9 = (bf16[96,768]{1,0:T(8,128)(2,1)S(1)}, bf16[96,768]{1,0:T(8,128)(2,1)S(1)}, u32[]{:S(2)}, u32[]{:S(2)}) collective-permute-start(bf16[96,768]{1,0:T(8,128)(2,1)S(1)} %get-tuple-element.42), channel_id=1, source_target_pairs={{0,1},{1,0},{2,3},{3,2},{4,5},{5,4},{6,7},{7,6},{8,9},{9,8},{10,11... | collective-permute-start | bytes 442376 | tf_op jit(solution)/shard_map/ppermute | solution.py:297
  52.3 2.8 %experts.7 = (bf16[96,768]{1,0:T(8,128)(2,1)S(1)}, bf16[96,768]{1,0:T(8,128)(2,1)S(1)}) custom-call(bf16[96,768]{1,0:T(8,128)(2,1)S(1)} %collective-permute-done.19.refs_0_, bf16[96,768]{1,0:T(8,128)(2,1)S(1)} %collective-permute-done.20.refs_1_, bf16[768,1536]{1,0:T(8,128)(2,1)S(1)} %bitcast.18, bf16[768,1536]{1,0:T(8,128)(2,1)S(1)} %bitcast.22, ...), custom_call_target="tpu_custom_call" | custom-call | flops 1358954496 | bytes 7667712 | tf_op jit(solution)/shard_map/experts/pallas_call | solution.py:183
  55.1 2.5 %collective-permute-start.21 = (bf16[96,768]{1,0:T(8,128)(2,1)S(1)}, bf16[96,768]{1,0:T(8,128)(2,1)S(1)}, u32[]{:S(2)}, u32[]{:S(2)}) collective-permute-start(bf16[96,768]{1,0:T(8,128)(2,1)S(1)} %get-tuple-element.55), channel_id=1, source_target_pairs={{0,6},{1,7},{2,4},{3,5},{4,2},{5,3},{6,0},{7,1},{8,14},{9,15},{10,... | collective-permute-start | bytes 442376 | tf_op jit(solution)/shard_map/ppermute | solution.py:297
  57.6 1.9 %collective-permute-start.22 = (bf16[96,768]{1,0:T(8,128)(2,1)S(1)}, bf16[96,768]{1,0:T(8,128)(2,1)S(1)}, u32[]{:S(2)}, u32[]{:S(2)}) collective-permute-start(bf16[96,768]{1,0:T(8,128)(2,1)S(1)} %get-tuple-element.56), channel_id=1, source_target_pairs={{0,7},{1,6},{2,5},{3,4},{4,3},{5,2},{6,1},{7,0},{8,15},{9,14},{10,... | collective-permute-start | bytes 442376 | tf_op jit(solution)/shard_map/ppermute | solution.py:297
  59.5 2.8 %experts.6 = (bf16[96,768]{1,0:T(8,128)(2,1)S(1)}, bf16[96,768]{1,0:T(8,128)(2,1)S(1)}) custom-call(bf16[96,768]{1,0:T(8,128)(2,1)S(1)} %collective-permute-done.15.refs_0_, bf16[96,768]{1,0:T(8,128)(2,1)S(1)} %collective-permute-done.16.refs_1_, bf16[768,1536]{1,0:T(8,128)(2,1)S(1)} %bitcast.19, bf16[768,1536]{1,0:T(8,128)(2,1)S(1)} %bitcast.23, ...), custom_call_target="tpu_custom_call" | custom-call | flops 1358954496 | bytes 7667712 | tf_op jit(solution)/shard_map/experts/pallas_call | solution.py:183
  63.7 2.8 %experts.5 = (bf16[96,768]{1,0:T(8,128)(2,1)S(1)}, bf16[96,768]{1,0:T(8,128)(2,1)S(1)}) custom-call(bf16[96,768]{1,0:T(8,128)(2,1)S(1)} %collective-permute-done.11.refs_0_, bf16[96,768]{1,0:T(8,128)(2,1)S(1)} %collective-permute-done.12.refs_1_, bf16[768,1536]{1,0:T(8,128)(2,1)S(1)} %bitcast.20, bf16[768,1536]{1,0:T(8,128)(2,1)S(1)} %bitcast.24, ...), custom_call_target="tpu_custom_call" | custom-call | flops 1358954496 | bytes 7667712 | tf_op jit(solution)/shard_map/experts/pallas_call | solution.py:183
  67.7 2.8 %experts.4 = (bf16[96,768]{1,0:T(8,128)(2,1)S(1)}, bf16[96,768]{1,0:T(8,128)(2,1)S(1)}) custom-call(bf16[96,768]{1,0:T(8,128)(2,1)S(1)} %get-tuple-element.41.refs_0_, bf16[96,768]{1,0:T(8,128)(2,1)S(1)} %collective-permute-done.9.refs_1_, bf16[768,1536]{1,0:T(8,128)(2,1)S(1)} %bitcast.21, bf16[768,1536]{1,0:T(8,128)(2,1)S(1)} %bitcast.25, ...), custom_call_target="tpu_custom_call" | custom-call | flops 1358954496 | bytes 7667712 | tf_op jit(solution)/shard_map/experts/pallas_call | solution.py:183
  71.9 4.7 %collective-permute-done.14.refs_3_ = bf16[96,768]{1,0:T(8,128)(2,1)S(1)} collective-permute-done((bf16[96,768]{1,0:T(8,128)(2,1)S(1)}, bf16[96,768]{1,0:T(8,128)(2,1)S(1)}, u32[]{:S(2)}, u32[]{:S(2)}) %collective-permute-start.14) | collective-permute-done | bytes 147488 | tf_op jit(solution)/shard_map/ppermute | solution.py:297
  76.6 1.6 %combine.1 = bf16[256,768]{1,0:T(8,128)(2,1)} custom-call(bf16[96,768]{1,0:T(8,128)(2,1)S(1)} %get-tuple-element.43.refs_0_, bf16[96,768]{1,0:T(8,128)(2,1)S(1)} %collective-permute-done.10.refs_1_, bf16[96,768]{1,0:T(8,128)(2,1)S(1)} %collective-permute-done.13.refs_2_, bf16[96,768]{1,0:T(8,128)(2,1)S(1)} %collective-permute-done.14.refs_3_, ...), custom_call_target="tpu_custom_call" | custom-call | flops 603979776 | bytes 1179648 | tf_op jit(solution)/shard_map/combine/pallas_call | solution.py:312
  (91 shorter events, 20.8 us)
Async XLA Ops:
  0.0 27.1 %copy-start.19 = (f32[24]{0:T(128)S(1)}, f32[24]{0:T(128)}, u32[]{:S(2)}) copy-start(f32[24]{0:T(128)} %param.25) | copy-start | bytes 292
  5.6 2.0 %collective-permute-start.4 = (bf16[128,512]{1,0:T(8,128)(2,1)S(1)}, bf16[128,512]{1,0:T(8,128)(2,1)S(1)}, u32[]{:S(2)}, u32[]{:S(2)}) collective-permute-start(bf16[128,512]{1,0:T(8,128)(2,1)S(1)} %get-tuple-element.35), channel_id=1, source_target_pairs={{0,8},{1,9},{2,10},{3,11},{4,12},{5,13},{6,14},{7,15}} | collective-permute-start | bytes 393224 | tf_op jit(solution)/shard_map/ppermute | solution.py:253
  6.3 2.7 %collective-permute-start.2 = (bf16[128,512]{1,0:T(8,128)(2,1)S(1)}, bf16[128,512]{1,0:T(8,128)(2,1)S(1)}, u32[]{:S(2)}, u32[]{:S(2)}) collective-permute-start(bf16[128,512]{1,0:T(8,128)(2,1)S(1)} %get-tuple-element.34), channel_id=1, source_target_pairs={{0,8},{1,9},{2,10},{3,11},{4,12},{5,13},{6,14},{7,15}} | collective-permute-start | bytes 393224 | tf_op jit(solution)/shard_map/ppermute | solution.py:253
  6.9 3.6 %collective-permute-start = (bf16[128,512]{1,0:T(8,128)(2,1)S(1)}, bf16[128,512]{1,0:T(8,128)(2,1)S(1)}, u32[]{:S(2)}, u32[]{:S(2)}) collective-permute-start(bf16[128,512]{1,0:T(8,128)(2,1)S(1)} %get-tuple-element.32), channel_id=1, source_target_pairs={{0,8},{1,9},{2,10},{3,11},{4,12},{5,13},{6,14},{7,15}} | collective-permute-start | bytes 393224 | tf_op jit(solution)/shard_map/ppermute | solution.py:253
  7.7 8.0 %collective-permute-start.5 = (bf16[128,512]{1,0:T(8,128)(2,1)S(1)}, bf16[128,512]{1,0:T(8,128)(2,1)S(1)}, u32[]{:S(2)}, u32[]{:S(2)}) collective-permute-start(bf16[128,512]{1,0:T(8,128)(2,1)S(1)} %fusion.4), channel_id=1, source_target_pairs={{8,16},{9,17},{10,18},{11,19},{12,20},{13,21},{14,22},{15,23}} | collective-permute-start | bytes 393224 | tf_op jit(solution)/shard_map/ppermute | solution.py:259
  9.1 11.1 %collective-permute-start.3 = (bf16[128,512]{1,0:T(8,128)(2,1)S(1)}, bf16[128,512]{1,0:T(8,128)(2,1)S(1)}, u32[]{:S(2)}, u32[]{:S(2)}) collective-permute-start(bf16[128,512]{1,0:T(8,128)(2,1)S(1)} %fusion.2), channel_id=1, source_target_pairs={{8,16},{9,17},{10,18},{11,19},{12,20},{13,21},{14,22},{15,23}} | collective-permute-start | bytes 393224 | tf_op jit(solution)/shard_map/ppermute | solution.py:259
  10.6 12.3 %collective-permute-start.1 = (bf16[128,512]{1,0:T(8,128)(2,1)S(1)}, bf16[128,512]{1,0:T(8,128)(2,1)S(1)}, u32[]{:S(2)}, u32[]{:S(2)}) collective-permute-start(bf16[128,512]{1,0:T(8,128)(2,1)S(1)} %fusion), channel_id=1, source_target_pairs={{8,16},{9,17},{10,18},{11,19},{12,20},{13,21},{14,22},{15,23}} | collective-permute-start | bytes 393224 | tf_op jit(solution)/shard_map/ppermute | solution.py:259
  16.4 19.0 %collective-permute-start.8 = (bf16[128,512]{1,0:T(8,128)(2,1)}, bf16[128,512]{1,0:T(8,128)(2,1)}, u32[]{:S(2)}, u32[]{:S(2)}) collective-permute-start(bf16[128,512]{1,0:T(8,128)(2,1)} %get-tuple-element.59), channel_id=1, source_target_pairs={{16,24},{17,25},{18,26},{19,27},{20,28},{21,29},{22,30},{23,31}} | collective-permute-start | bytes 393224 | tf_op jit(solution)/shard_map/ppermute | solution.py:259
  20.9 14.6 %collective-permute-start.7 = (bf16[128,512]{1,0:T(8,128)(2,1)}, bf16[128,512]{1,0:T(8,128)(2,1)}, u32[]{:S(2)}, u32[]{:S(2)}) collective-permute-start(bf16[128,512]{1,0:T(8,128)(2,1)} %get-tuple-element.61), channel_id=1, source_target_pairs={{16,24},{17,25},{18,26},{19,27},{20,28},{21,29},{22,30},{23,31}} | collective-permute-start | bytes 393224 | tf_op jit(solution)/shard_map/ppermute | solution.py:259
  23.6 11.9 %collective-permute-start.6 = (bf16[128,512]{1,0:T(8,128)(2,1)}, bf16[128,512]{1,0:T(8,128)(2,1)}, u32[]{:S(2)}, u32[]{:S(2)}) collective-permute-start(bf16[128,512]{1,0:T(8,128)(2,1)} %get-tuple-element.63), channel_id=1, source_target_pairs={{16,24},{17,25},{18,26},{19,27},{20,28},{21,29},{22,30},{23,31}} | collective-permute-start | bytes 393224 | tf_op jit(solution)/shard_map/ppermute | solution.py:259
  39.0 8.3 %collective-permute-start.19 = (bf16[96,768]{1,0:T(8,128)(2,1)S(1)}, bf16[96,768]{1,0:T(8,128)(2,1)S(1)}, u32[]{:S(2)}, u32[]{:S(2)}) collective-permute-start(bf16[96,768]{1,0:T(8,128)(2,1)S(1)} %get-tuple-element.53), channel_id=1, source_target_pairs={{0,6},{1,7},{2,4},{3,5},{4,2},{5,3},{6,0},{7,1},{8,14},{9,15},{10,... | collective-permute-start | bytes 442376 | tf_op jit(solution)/shard_map/ppermute | solution.py:297
  41.3 9.6 %collective-permute-start.20 = (bf16[96,768]{1,0:T(8,128)(2,1)S(1)}, bf16[96,768]{1,0:T(8,128)(2,1)S(1)}, u32[]{:S(2)}, u32[]{:S(2)}) collective-permute-start(bf16[96,768]{1,0:T(8,128)(2,1)S(1)} %get-tuple-element.54), channel_id=1, source_target_pairs={{0,7},{1,6},{2,5},{3,4},{4,3},{5,2},{6,1},{7,0},{8,15},{9,14},{10,... | collective-permute-start | bytes 442376 | tf_op jit(solution)/shard_map/ppermute | solution.py:297
  44.9 10.2 %collective-permute-start.15 = (bf16[96,768]{1,0:T(8,128)(2,1)S(1)}, bf16[96,768]{1,0:T(8,128)(2,1)S(1)}, u32[]{:S(2)}, u32[]{:S(2)}) collective-permute-start(bf16[96,768]{1,0:T(8,128)(2,1)S(1)} %get-tuple-element.49), channel_id=1, source_target_pairs={{0,4},{1,5},{2,6},{3,7},{4,0},{5,1},{6,2},{7,3},{8,12},{9,13},{10,... | collective-permute-start | bytes 442376 | tf_op jit(solution)/shard_map/ppermute | solution.py:297
  46.1 11.5 %collective-permute-start.16 = (bf16[96,768]{1,0:T(8,128)(2,1)S(1)}, bf16[96,768]{1,0:T(8,128)(2,1)S(1)}, u32[]{:S(2)}, u32[]{:S(2)}) collective-permute-start(bf16[96,768]{1,0:T(8,128)(2,1)S(1)} %get-tuple-element.50), channel_id=1, source_target_pairs={{0,5},{1,4},{2,7},{3,6},{4,1},{5,0},{6,3},{7,2},{8,13},{9,12},{10,... | collective-permute-start | bytes 442376 | tf_op jit(solution)/shard_map/ppermute | solution.py:297
  46.4 15.9 %collective-permute-start.11 = (bf16[96,768]{1,0:T(8,128)(2,1)S(1)}, bf16[96,768]{1,0:T(8,128)(2,1)S(1)}, u32[]{:S(2)}, u32[]{:S(2)}) collective-permute-start(bf16[96,768]{1,0:T(8,128)(2,1)S(1)} %get-tuple-element.45), channel_id=1, source_target_pairs={{0,2},{1,3},{2,0},{3,1},{4,6},{5,7},{6,4},{7,5},{8,10},{9,11},{10,... | collective-permute-start | bytes 442376 | tf_op jit(solution)/shard_map/ppermute | solution.py:297
  47.3 15.7 %collective-permute-start.12 = (bf16[96,768]{1,0:T(8,128)(2,1)S(1)}, bf16[96,768]{1,0:T(8,128)(2,1)S(1)}, u32[]{:S(2)}, u32[]{:S(2)}) collective-permute-start(bf16[96,768]{1,0:T(8,128)(2,1)S(1)} %get-tuple-element.46), channel_id=1, source_target_pairs={{0,3},{1,2},{2,1},{3,0},{4,7},{5,6},{6,5},{7,4},{8,11},{9,10},{10,... | collective-permute-start | bytes 442376 | tf_op jit(solution)/shard_map/ppermute | solution.py:297
  50.9 15.7 %collective-permute-start.9 = (bf16[96,768]{1,0:T(8,128)(2,1)S(1)}, bf16[96,768]{1,0:T(8,128)(2,1)S(1)}, u32[]{:S(2)}, u32[]{:S(2)}) collective-permute-start(bf16[96,768]{1,0:T(8,128)(2,1)S(1)} %get-tuple-element.42), channel_id=1, source_target_pairs={{0,1},{1,0},{2,3},{3,2},{4,5},{5,4},{6,7},{7,6},{8,9},{9,8},{10,11... | collective-permute-start | bytes 442376 | tf_op jit(solution)/shard_map/ppermute | solution.py:297
  55.1 15.4 %collective-permute-start.21 = (bf16[96,768]{1,0:T(8,128)(2,1)S(1)}, bf16[96,768]{1,0:T(8,128)(2,1)S(1)}, u32[]{:S(2)}, u32[]{:S(2)}) collective-permute-start(bf16[96,768]{1,0:T(8,128)(2,1)S(1)} %get-tuple-element.55), channel_id=1, source_target_pairs={{0,6},{1,7},{2,4},{3,5},{4,2},{5,3},{6,0},{7,1},{8,14},{9,15},{10,... | collective-permute-start | bytes 442376 | tf_op jit(solution)/shard_map/ppermute | solution.py:297
  57.6 14.1 %collective-permute-start.22 = (bf16[96,768]{1,0:T(8,128)(2,1)S(1)}, bf16[96,768]{1,0:T(8,128)(2,1)S(1)}, u32[]{:S(2)}, u32[]{:S(2)}) collective-permute-start(bf16[96,768]{1,0:T(8,128)(2,1)S(1)} %get-tuple-element.56), channel_id=1, source_target_pairs={{0,7},{1,6},{2,5},{3,4},{4,3},{5,2},{6,1},{7,0},{8,15},{9,14},{10,... | collective-permute-start | bytes 442376 | tf_op jit(solution)/shard_map/ppermute | solution.py:297
  62.3 9.5 %collective-permute-start.17 = (bf16[96,768]{1,0:T(8,128)(2,1)S(1)}, bf16[96,768]{1,0:T(8,128)(2,1)S(1)}, u32[]{:S(2)}, u32[]{:S(2)}) collective-permute-start(bf16[96,768]{1,0:T(8,128)(2,1)S(1)} %get-tuple-element.51), channel_id=1, source_target_pairs={{0,4},{1,5},{2,6},{3,7},{4,0},{5,1},{6,2},{7,3},{8,12},{9,13},{10,... | collective-permute-start | bytes 442376 | tf_op jit(solution)/shard_map/ppermute | solution.py:297
  63.1 8.8 %collective-permute-start.18 = (bf16[96,768]{1,0:T(8,128)(2,1)S(1)}, bf16[96,768]{1,0:T(8,128)(2,1)S(1)}, u32[]{:S(2)}, u32[]{:S(2)}) collective-permute-start(bf16[96,768]{1,0:T(8,128)(2,1)S(1)} %get-tuple-element.52), channel_id=1, source_target_pairs={{0,5},{1,4},{2,7},{3,6},{4,1},{5,0},{6,3},{7,2},{8,13},{9,12},{10,... | collective-permute-start | bytes 442376 | tf_op jit(solution)/shard_map/ppermute | solution.py:297
  66.5 5.4 %collective-permute-start.13 = (bf16[96,768]{1,0:T(8,128)(2,1)S(1)}, bf16[96,768]{1,0:T(8,128)(2,1)S(1)}, u32[]{:S(2)}, u32[]{:S(2)}) collective-permute-start(bf16[96,768]{1,0:T(8,128)(2,1)S(1)} %get-tuple-element.47), channel_id=1, source_target_pairs={{0,2},{1,3},{2,0},{3,1},{4,6},{5,7},{6,4},{7,5},{8,10},{9,11},{10,... | collective-permute-start | bytes 442376 | tf_op jit(solution)/shard_map/ppermute | solution.py:297
  70.5 6.1 %collective-permute-start.14 = (bf16[96,768]{1,0:T(8,128)(2,1)S(1)}, bf16[96,768]{1,0:T(8,128)(2,1)S(1)}, u32[]{:S(2)}, u32[]{:S(2)}) collective-permute-start(bf16[96,768]{1,0:T(8,128)(2,1)S(1)} %get-tuple-element.48), channel_id=1, source_target_pairs={{0,3},{1,2},{2,1},{3,0},{4,7},{5,6},{6,5},{7,4},{8,11},{9,10},{10,... | collective-permute-start | bytes 442376 | tf_op jit(solution)/shard_map/ppermute | solution.py:297
  71.7 4.8 %collective-permute-start.10 = (bf16[96,768]{1,0:T(8,128)(2,1)S(1)}, bf16[96,768]{1,0:T(8,128)(2,1)S(1)}, u32[]{:S(2)}, u32[]{:S(2)}) collective-permute-start(bf16[96,768]{1,0:T(8,128)(2,1)S(1)} %get-tuple-element.44), channel_id=1, source_target_pairs={{0,1},{1,0},{2,3},{3,2},{4,5},{5,4},{6,7},{7,6},{8,9},{9,8},{10,11... | collective-permute-start | bytes 442376 | tf_op jit(solution)/shard_map/ppermute | solution.py:297
  (24 other events, 214.7 us)

commit v2 on v1

v2 whole, which is shorter than its diff:
```python
import functools

import jax
import jax.numpy as jnp
from jax import lax
from jax.experimental import pallas as pl
from jax.experimental.pallas import tpu as pltpu
from jax.sharding import PartitionSpec as P

EPS = 1e-05
F32 = jnp.float32
BF16 = jnp.bfloat16
CHUNKS = 3
K2_MIB = 32


def call(body, name, out_shape, flops, nbytes, mib=32, **kwargs):
    return pl.pallas_call(
        body,
        out_shape=out_shape,
        name=name,
        compiler_params=pltpu.CompilerParams(vmem_limit_bytes=mib * 2**20),
        cost_estimate=pl.CostEstimate(flops=flops, bytes_accessed=nbytes, transcendentals=0),
        **kwargs,
    )


def dot(a, b):
    return jnp.dot(a, b, preferred_element_type=F32)


def dot_rows(a, b):
    return lax.dot_general(a, b, (((0,), (0,)), ((), ())), preferred_element_type=F32)


def pieces(value, count):
    parts = []
    for _ in range(count):
        part = value.astype(BF16)
        parts.append(part)
        value = value - part.astype(F32)
    return parts


def iota(shape, dim):
    return lax.broadcasted_iota(jnp.int32, shape, dim)


def fetch(sources, buffers, sems):
    copies = [pltpu.make_async_copy(s, b, sems.at[i]) for i, (s, b) in enumerate(zip(sources, buffers))]
    for copy in copies:
        copy.start()
    return copies


def parts_of(ref, count):
    width = ref.shape[1] // count
    return [ref.at[:, k * width : (k + 1) * width] for k in range(count)]


def lead_kernel(*refs):
    @pl.when(lax.axis_index("seq") == 0)
    def _():
        block_state(refs[:5], (), (), refs[5 : 5 + CHUNKS], refs[5 + CHUNKS :])


def state_kernel(*refs):
    block_state(refs[:5], refs[5:7], refs[7 : 7 + CHUNKS], refs[7 + CHUNKS : 7 + 2 * CHUNKS], refs[7 + 2 * CHUNKS :])


def block_state(arrays, step_refs, decay_refs, state_refs, scratch):
    dt_hbm, bias_hbm, alog_hbm, x_hbm, write_hbm = arrays
    dt_ref, bias_ref, alog_ref, x_ref, write_ref, sems = scratch
    length, inner = x_ref.shape
    heads = dt_ref.shape[0]
    copies = fetch(
        [dt_hbm, bias_hbm, alog_hbm, write_hbm] + parts_of(x_hbm, CHUNKS),
        [dt_ref, bias_ref, alog_ref, write_ref] + parts_of(x_ref, CHUNKS),
        sems,
    )
    lower = (iota((length, length), 0) >= iota((length, length), 1)).astype(F32).astype(BF16)
    expand = (iota((heads, inner), 1) // (inner // heads) == iota((heads, inner), 0)).astype(F32).astype(BF16)
    for copy in copies[:3]:
        copy.wait()
    raw = dt_ref[...].T + bias_ref[...]
    step = jnp.maximum(raw, 0.0) + jnp.log1p(jnp.exp(-jnp.abs(raw)))
    log_decay = -jnp.exp(alog_ref[...]) * step
    cum = sum(dot(lower, part) for part in pieces(log_decay, 3))
    last = cum[length - 1 : length, :]
    to_end = jnp.exp(jnp.minimum(last - cum, 0.0)) * step
    if step_refs:
        decay = sum(dot(part, expand) for part in pieces(jnp.broadcast_to(jnp.exp(last), (8, heads)), 3))
        step_refs[0][...] = cum
        step_refs[1][...] = step
    ends = pieces(to_end, 2)
    width = inner // CHUNKS
    copies[3].wait()
    for k in range(CHUNKS):
        cols = slice(k * width, (k + 1) * width)
        if step_refs:
            decay_refs[k][...] = decay[0:1, cols]
        wide = sum(dot(part, expand[:, cols]) for part in ends)
        copies[4 + k].wait()
        scaled = (x_ref[:, cols].astype(F32) * wide).astype(BF16)
        state_refs[k][...] = dot_rows(write_ref[...], scaled).astype(BF16)


def intra_kernel(xor, capacity, cum_ref, step_ref, x_ref, gate_ref, write_ref, read_ref, skip_ref, ids_ref,
                 own_ref, factor_ref, route_ref, target_ref):
    length, inner = x_ref.shape
    experts = route_ref.shape[0] // capacity
    hits = [(ids_ref[k : k + 1, :] == iota((experts, length), 0)).astype(F32) for k in range(2)]
    earlier = (iota((length, length), 0) < iota((length, length), 1)).astype(F32).astype(BF16)
    before = dot((hits[0] + hits[1]).astype(BF16), earlier)
    rows = jnp.zeros(route_ref.shape, F32)
    for k in range(2):
        slot = jnp.sum(before * hits[k], axis=0, keepdims=True).astype(jnp.int32)
        owner = ids_ref[k : k + 1, :]
        if xor:
            owner = owner ^ lax.axis_index("exp")
        target = owner * capacity + slot
        target_ref[k : k + 1, :] = target.astype(F32)
        rows = jnp.where(target == iota(route_ref.shape, 0), 1.0, rows)
    route_ref[...] = rows.astype(BF16)
    heads = cum_ref.shape[1]
    half = length // 2
    cum = cum_ref[...]
    cum_rows = cum.T
    step_rows = step_ref[...].T
    scores = lax.dot_general(
        read_ref[...], write_ref[...], (((1,), (1,)), ((), ())), preferred_element_type=F32
    )
    scores = jnp.where(iota((length, length), 0) >= iota((length, length), 1), scores, 0.0)
    lanes = 2 * (inner // heads)
    first = iota((length, lanes), 1) < lanes // 2
    first_row = iota((1, lanes), 1) < lanes // 2
    for pair in range(heads // 2):
        cols = slice(pair * lanes, (pair + 1) * lanes)
        x = x_ref[:, cols]
        wide = x.astype(F32)
        masked = [jnp.where(first, wide, 0.0).astype(BF16), jnp.where(first, 0.0, wide).astype(BF16)]
        tops, bottoms = [], []
        for h in (2 * pair, 2 * pair + 1):
            here = cum[:, h : h + 1]
            there = cum_rows[h : h + 1, :]
            steps = step_rows[h : h + 1, :]
            top = jnp.exp(jnp.minimum(here[:half] - there[:, :half], 0.0))
            tops.append((scores[:half, :half] * top * steps[:, :half]).astype(BF16))
            bottom = jnp.exp(jnp.minimum(here[half:] - there, 0.0))
            bottoms.append((scores[half:, :] * bottom * steps).astype(BF16))
        y_top = dot(jnp.concatenate(tops, 1), jnp.concatenate([m[:half] for m in masked], 0))
        y_bottom = dot(jnp.concatenate(bottoms, 1), jnp.concatenate(masked, 0))
        y = jnp.concatenate([y_top, y_bottom], 0)
        skip = jnp.where(first_row, skip_ref[:, 2 * pair : 2 * pair + 1], skip_ref[:, 2 * pair + 1 : 2 * pair + 2])
        gate = gate_ref[:, cols].astype(F32)
        gate = gate / (1.0 + jnp.exp(-gate))
        grown = jnp.exp(jnp.where(first, cum[:, 2 * pair : 2 * pair + 1], cum[:, 2 * pair + 1 : 2 * pair + 2]))
        own_ref[:, cols] = ((y + skip * wide) * gate).astype(own_ref.dtype)
        factor_ref[:, cols] = (grown * gate).astype(factor_ref.dtype)


def mix_kernel(chunks, *refs):
    earlier, latest = refs[:chunks], refs[chunks : 2 * chunks]
    (read_ref, own_ref, factor_ref, norm_ref, weight_ref, hidden_ref, gain_ref, route_ref) = refs[2 * chunks : 2 * chunks + 8]
    stream_ref, *buffer_refs, mixed_ref = refs[2 * chunks + 8 :]
    inner = own_ref.shape[1]
    width = inner // chunks
    total = 0.0
    for k in range(chunks):
        cols = slice(k * width, (k + 1) * width)
        incoming = (earlier[k][...].astype(F32) + latest[k][...].astype(F32)).astype(BF16)
        value = own_ref[:, cols] + factor_ref[:, cols] * dot(read_ref[...], incoming)
        mixed_ref[:, cols] = value
        total = total + jnp.sum(value * value, axis=1, keepdims=True)
    scale = lax.rsqrt(total / inner + EPS)
    gated = (mixed_ref[...] * scale * norm_ref[...]).astype(BF16)
    stream = hidden_ref[...].astype(F32) + dot(gated, weight_ref[...])
    stream_ref[...] = stream
    scale = lax.rsqrt(jnp.mean(stream * stream, axis=1, keepdims=True) + EPS)
    normed = (stream * scale * gain_ref[...]).astype(BF16)
    at = 0
    for buffer_ref in buffer_refs:
        rows = buffer_ref.shape[0]
        buffer_ref[...] = dot(route_ref[at : at + rows, :], normed).astype(BF16)
        at += rows


def expert_kernel(count, *refs):
    rows, (gate_ref, up_ref, down_ref), outs = refs[:count], refs[count : count + 3], refs[count + 3 :]
    x = jnp.concatenate([r[...] for r in rows], 0)
    hidden = gate_ref.shape[1]
    tile = hidden // 3
    total = 0.0
    for k in range(3):
        cols = slice(k * tile, (k + 1) * tile)
        gate = dot(x, gate_ref[:, cols])
        active = (gate / (1.0 + jnp.exp(-gate)) * dot(x, up_ref[:, cols])).astype(BF16)
        total = total + dot(active, down_ref[cols, :])
    at = 0
    for out in outs:
        out[...] = total[at : at + out.shape[0], :].astype(BF16)
        at += out.shape[0]


def run_expert(rows, w_gate, w_up, w_down):
    width = w_gate.shape[0]
    sizes = [r.shape[0] for r in rows]
    return call(
        functools.partial(expert_kernel, len(rows)),
        "experts",
        [jax.ShapeDtypeStruct((n, width), BF16) for n in sizes],
        sum(sizes),
        sum(sizes),
    )(*rows, w_gate, w_up, w_down)


def combine_kernel(order, *refs):
    count = len(order)
    rows, (target_ref, values_ref, stream_ref, out_ref) = refs[:count], refs[count:]
    returned = jnp.concatenate([rows[order.index(k)][...] for k in range(count)], 0)
    total = stream_ref[...]
    length = total.shape[0]
    columns = jnp.concatenate([target_ref[...], values_ref[...], jnp.zeros((4, length), F32)], 0).T
    for k in range(2):
        target = columns[:, k : k + 1].astype(jnp.int32)
        pick = (target == iota((length, returned.shape[0]), 1)).astype(F32).astype(BF16)
        total = total + columns[:, 2 + k : 3 + k] * dot(pick, returned)
    out_ref[...] = total.astype(BF16)


def on_device(
    hidden,
    ssm_input,
    ssm_gate,
    write_proj,
    read_proj,
    dt_raw,
    dt_bias,
    a_log,
    d_skip,
    norm_gain,
    out_weight,
    moe_gain,
    expert_ids,
    gate_values,
    w_gate,
    w_up,
    w_down,
):
    signal, gate, write, read = ssm_input[0], ssm_gate[0], write_proj[0], read_proj[0]
    length, inner = signal.shape
    width = hidden.shape[2]
    heads, state = dt_raw.shape[1], write.shape[1]
    n_seq, n_exp = lax.axis_size("seq"), lax.axis_size("exp")
    experts = n_exp * w_gate.shape[0]
    capacity = max(2, 3 * length // experts)
    slots = experts * capacity
    direct = n_exp == 8 and capacity % 16 == 0 and w_gate.shape[0] == 1
    shape = jax.ShapeDtypeStruct

    part = inner // CHUNKS
    operands = (dt_raw[0], dt_bias[None], a_log[None], signal, write)
    state_shapes = [shape((state, part), BF16)] * CHUNKS
    state_call = dict(
        mib=60,
        in_specs=[pl.BlockSpec(memory_space=pltpu.HBM)] * 5,
        scratch_shapes=[
            pltpu.VMEM((heads, length), F32),
            pltpu.VMEM((1, heads), F32),
            pltpu.VMEM((1, heads), F32),
            pltpu.VMEM((length, inner), BF16),
            pltpu.VMEM((length, state), BF16),
            pltpu.SemaphoreType.DMA((4 + CHUNKS,)),
        ],
    )
    work = (2 * length * state * inner, 2 * length * inner)
    lead = call(lead_kernel, "first_state", state_shapes, *work, **state_call)(*operands)
    received = [lax.ppermute(s, "seq", [(0, 1)]) for s in lead]
    dt_own, _ = lax.optimization_barrier((dt_raw[0], lead[0]))
    cum, step, *chain = call(
        state_kernel,
        "block_state",
        [shape((length, heads), F32)] * 2 + [shape((1, part), F32)] * CHUNKS + state_shapes,
        *work,
        **state_call,
    )(dt_own, *operands[1:])

    decays, states = chain[:CHUNKS], chain[CHUNKS:]
    incoming = [jnp.zeros_like(s) for s in states]
    received[0], cum = lax.optimization_barrier((received[0], cum))
    def intra(cum):
        return call(
            functools.partial(intra_kernel, direct, capacity),
            "intra_block",
            [
                shape((length, inner), F32),
                shape((length, inner), F32),
                shape((slots, length), BF16),
                shape((2, length), F32),
            ],
            4 * length * length * inner,
            12 * length * inner,
            mib=K2_MIB,
        )(cum, step, signal, gate, write, read, d_skip[None], expert_ids[0].T)

    for hop in range(2, n_seq):
        for k in range(CHUNKS):
            incoming[k] = incoming[k] + received[k] if hop > 2 else received[k]
            sent = decays[k] * incoming[k].astype(F32) + states[k].astype(F32)
            sent, incoming[k] = lax.optimization_barrier((sent.astype(BF16), incoming[k]))
            received[k] = lax.ppermute(sent, "seq", [(hop - 1, hop)])
        if hop == 2:
            cum, sent = lax.optimization_barrier((cum, sent))
            own, factor, route, targets = intra(cum)
            received[0], own = lax.optimization_barrier((received[0], own))

    blocks = [capacity] * n_exp if direct else [slots]
    stream, *buffers = call(
        functools.partial(mix_kernel, CHUNKS),
        "mix",
        [shape((length, width), F32)] + [shape((n, width), BF16) for n in blocks],
        2 * length * inner * width,
        8 * length * inner,
        scratch_shapes=[pltpu.VMEM((length, inner), F32)],
    )(
        *incoming,
        *received,
        read,
        own,
        factor,
        norm_gain[None],
        out_weight,
        hidden[0],
        moe_gain[None],
        route,
    )

    weights = (w_gate[0], w_up[0], w_down[0])
    if direct:
        swap = lambda rows, k: lax.ppermute(rows, "exp", [(i, i ^ k) for i in range(n_exp)])
        arrived = [buffers[0]] + [None] * (n_exp - 1)
        returned = [None] * n_exp
        for k in (1, 6, 7, 2, 4, 3, 5):
            arrived[k] = swap(buffers[k], k)
        before = None
        groups = ((0, 1), (6, 7), (2, 4), (3, 5))
        order = [k for group in groups for k in group]
        for group in groups:
            rows = [arrived[k] for k in group]
            if before is not None:
                *rows, before = lax.optimization_barrier((*rows, before))
            results = run_expert(rows, *weights)
            before = results[0]
            for k, rows in zip(group, results):
                returned[k] = rows if k == 0 else swap(rows, k)
    else:
        trade = lambda rows: lax.all_to_all(
            rows.reshape(n_exp, -1, width), "exp", split_axis=0, concat_axis=0, tiled=True
        ).reshape(-1, width)
        order = [0]
        returned = [trade(run_expert([trade(buffers[0])], *weights)[0])]

    total = call(
        functools.partial(combine_kernel, order),
        "combine",
        shape((length, width), BF16),
        4 * length * slots * width,
        2 * slots * width,
    )(*[returned[k] for k in order], targets, gate_values[0].T, stream)
    return total[None]


def solution(mesh):
    in_specs = (
        P("exp", "seq", None),
        P("exp", "seq", None),
        P("exp", "seq", None),
        P("exp", "seq", None),
        P("exp", "seq", None),
        P("exp", None, "seq"),
        P(),
        P(),
        P(),
        P(),
        P(),
        P(),
        P("exp", "seq", None),
        P("exp", "seq", None),
        P("exp", None, None),
        P("exp", None, None),
        P("exp", None, None),
    )
    out_specs = P("exp", "seq", None)
    return jax.shard_map(
        on_device, mesh=mesh, in_specs=in_specs, out_specs=out_specs, check_vma=False
    )
```

time: 78.7 us -> 64.3 us (0.82)
  local copies, waits for them, and re-layouts: 11.2 us -> 1.91 us
  starting transfers between devices: 32.6 us -> 26.3 us
  waiting for transfers between devices: 11 us -> 13.7 us
  Pallas kernels: 20.7 us -> 18.2 us
    unnamed x52 -> x44, local copies, waits for them, and re-layouts: 11.2 us -> 1.89 us
    ppermute x14, starting transfers between devices: 20.7 us -> 16.3 us  [on_device(): lax.ppermute(rows, 'exp', [(i, i ^ k) for i in range(n_exp)])]
    ppermute x14, waiting for transfers between devices: 5.27 us -> 8.23 us  [on_device(): lax.ppermute(rows, 'exp', [(i, i ^ k) for i in range(n_exp)])]
    ppermute x6, starting transfers between devices: 9.85 us -> 7.99 us  [on_device(): received[k] = lax.ppermute(sent, 'seq', [(hop - 1, hop)])]
    pallas_call x7 -> x8, Pallas kernels: 17.2 us -> 15.9 us  [the longest x4 7.3 us: run_expert(): call(functools.partial(expert_kernel, len(rows)), 'experts', [jax.ShapeDt...]
    pallas_call x1, Pallas kernels: 3.45 us -> 2.32 us  [on_device(): call(functools.partial(mix_kernel, CHUNKS), 'mix', [shape((length, width)...]
    convert_element_type x6 -> x5, other arithmetic: 2.29 us -> 2.5 us  [on_device(): sent.astype(BF16)]
  transfers between devices with their start and end apart: 23 -> 23, of which waited for: 4 -> 9; matrix products, arithmetic and copies ran while one was open for 5% -> 4% of each run, Pallas kernels for 18% -> 21%
where the time goes in v2:
time: 64.3 us; the launch traced here: 63.1 us
  starting transfers between devices  26.3 us (41%)
  Pallas kernels  18.2 us (28%)
  waiting for transfers between devices  13.7 us (21%)
  other arithmetic  2.5 us (4%)
  local copies, waits for them, and re-layouts  1.91 us (3%)
    ppermute x14, starting transfers between devices, on_device(): lax.ppermute(rows, 'exp', [(i, i ^ k) for i in range(n_exp)])  16.3 us
    ppermute x14, waiting for transfers between devices, on_device(): lax.ppermute(rows, 'exp', [(i, i ^ k) for i in range(n_exp)])  8.23 us
    ppermute x6, starting transfers between devices, on_device(): received[k] = lax.ppermute(sent, 'seq', [(hop - 1, hop)])  7.99 us
    pallas_call x4, Pallas kernels, run_expert(): call(functools.partial(expert_kernel, len(rows)), 'experts', [jax.ShapeDt...  7.3 us
    ppermute x6, waiting for transfers between devices, on_device(): received[k] = lax.ppermute(sent, 'seq', [(hop - 1, hop)])  5.42 us
    pallas_call x1, Pallas kernels, on_device(): call(state_kernel, 'block_state', [shape((length, heads), F32)] * 2 + [sh...  3.29 us
    pallas_call x1, Pallas kernels, intra(): call(functools.partial(intra_kernel, direct, capacity), 'intra_block', [s...  2.64 us
    convert_element_type x5, other arithmetic, on_device(): sent.astype(BF16)  2.5 us
  transfers between devices with their start and end apart: 23, of which 9 were waited for; matrix products, arithmetic and copies ran while one was open for 4% of the time, Pallas kernels for 21%

profile of v2, /device:TPU:17, one launch (start us, length us, event | category | flops | bytes accessed | tf_op | source)
XLA Modules:
  0.0 63.1 jit_solution(7073777667009661174)
XLA Ops:
  2.9 3.3 %block_state.1 = (f32[256,24]{1,0:T(8,128)}, f32[256,24]{1,0:T(8,128)}, f32[1,512]{1,0:T(1,128)}, f32[1,512]{1,0:T(1,128)}, f32[1,512]{1,0:T(1,128)}, /*index=5*...) custom-call(f32[24,256]{1,0:T(8,128)} %bitcast.48, f32[1,24]{1,0:T(1,128)} %bitcast.56, ...), custom_call_target="tpu_custom_call" | custom-call | flops 100663296 | bytes 786432 | tf_op jit(solution)/shard_map/block_state/pallas_call | solution.py:280
  7.4 1.3 %collective-permute-start.4 = (bf16[128,512]{1,0:T(8,128)(2,1)S(1)}, bf16[128,512]{1,0:T(8,128)(2,1)S(1)}, u32[]{:S(2)}, u32[]{:S(2)}) collective-permute-start(bf16[128,512]{1,0:T(8,128)(2,1)S(1)} %fusion.4), channel_id=1, source_target_pairs={{8,16},{9,17},{10,18},{11,19},{12,20},{13,21},{14,22},{15,23}} | collective-permute-start | bytes 393224 | tf_op jit(solution)/shard_map/ppermute | solution.py:311
  10.0 1.3 %collective-permute-start.5 = (bf16[128,512]{1,0:T(8,128)(2,1)S(1)}, bf16[128,512]{1,0:T(8,128)(2,1)S(1)}, u32[]{:S(2)}, u32[]{:S(2)}) collective-permute-start(bf16[128,512]{1,0:T(8,128)(2,1)S(1)} %get-tuple-element.73), channel_id=1, source_target_pairs={{8,16},{9,17},{10,18},{11,19},{12,20},{13,21},{14,22},{15,23}} | collective-permute-start | bytes 393224 | tf_op jit(solution)/shard_map/ppermute | solution.py:311
  11.3 1.3 %collective-permute-start.1 = (bf16[128,512]{1,0:T(8,128)(2,1)S(1)}, bf16[128,512]{1,0:T(8,128)(2,1)S(1)}, u32[]{:S(2)}, u32[]{:S(2)}) collective-permute-start(bf16[128,512]{1,0:T(8,128)(2,1)S(1)} %get-tuple-element.68), channel_id=1, source_target_pairs={{8,16},{9,17},{10,18},{11,19},{12,20},{13,21},{14,22},{15,23}} | collective-permute-start | bytes 393224 | tf_op jit(solution)/shard_map/ppermute | solution.py:311
  14.4 2.6 %intra_block.1 = (f32[256,1536]{1,0:T(8,128)S(1)}, f32[256,1536]{1,0:T(8,128)S(1)}, bf16[768,256]{1,0:T(8,128)(2,1)S(1)}, f32[2,256]{1,0:T(2,128)S(1)}) custom-call(f32[256,24]{1,0:T(8,128)S(1)} %copy-done.9, f32[256,24]{1,0:T(8,128)S(1)} %copy-done.10, bf16[256,1536]{1,0:T(8,128)(2,1)S(1)} %bitcast.36, bf16[256,1536]{1,0:T(8,128)(2,1)S(1)} %bitcast.37, ...), custom_call_target="tpu_custom_call" | custom-call | flops 402653184 | bytes 4718592 | tf_op jit(solution)/shard_map/intra_block/pallas_call | solution.py:292
  17.2 1.3 %collective-permute-start.7 = (bf16[128,512]{1,0:T(8,128)(2,1)S(1)}, bf16[128,512]{1,0:T(8,128)(2,1)S(1)}, u32[]{:S(2)}, u32[]{:S(2)}) collective-permute-start(bf16[128,512]{1,0:T(8,128)(2,1)S(1)} %get-tuple-element.88), channel_id=1, source_target_pairs={{16,24},{17,25},{18,26},{19,27},{20,28},{21,29},{22,30},{23,31}} | collective-permute-start | bytes 393224 | tf_op jit(solution)/shard_map/ppermute | solution.py:311
  19.8 1.3 %collective-permute-start.8 = (bf16[128,512]{1,0:T(8,128)(2,1)S(1)}, bf16[128,512]{1,0:T(8,128)(2,1)S(1)}, u32[]{:S(2)}, u32[]{:S(2)}) collective-permute-start(bf16[128,512]{1,0:T(8,128)(2,1)S(1)} %get-tuple-element.89), channel_id=1, source_target_pairs={{16,24},{17,25},{18,26},{19,27},{20,28},{21,29},{22,30},{23,31}} | collective-permute-start | bytes 393224 | tf_op jit(solution)/shard_map/ppermute | solution.py:311
  21.1 1.4 %collective-permute-done.1 = bf16[128,512]{1,0:T(8,128)(2,1)S(1)} collective-permute-done((bf16[128,512]{1,0:T(8,128)(2,1)S(1)}, bf16[128,512]{1,0:T(8,128)(2,1)S(1)}, u32[]{:S(2)}, u32[]{:S(2)}) %collective-permute-start.1) | collective-permute-done | bytes 131104 | tf_op jit(solution)/shard_map/ppermute | solution.py:311
  22.6 1.5 %collective-permute-start.6 = (bf16[128,512]{1,0:T(8,128)(2,1)S(1)}, bf16[128,512]{1,0:T(8,128)(2,1)S(1)}, u32[]{:S(2)}, u32[]{:S(2)}) collective-permute-start(bf16[128,512]{1,0:T(8,128)(2,1)S(1)} %get-tuple-element.87), channel_id=1, source_target_pairs={{16,24},{17,25},{18,26},{19,27},{20,28},{21,29},{22,30},{23,31}} | collective-permute-start | bytes 393224 | tf_op jit(solution)/shard_map/ppermute | solution.py:311
  24.2 2.8 %collective-permute-done.6.refs_3_ = bf16[128,512]{1,0:T(8,128)(2,1)S(1)} collective-permute-done((bf16[128,512]{1,0:T(8,128)(2,1)S(1)}, bf16[128,512]{1,0:T(8,128)(2,1)S(1)}, u32[]{:S(2)}, u32[]{:S(2)}) %collective-permute-start.6) | collective-permute-done | bytes 131104 | tf_op jit(solution)/shard_map/ppermute | solution.py:311
  27.0 2.3 %mix.1 = (f32[256,768]{1,0:T(8,128)S(1)}, bf16[96,768]{1,0:T(8,128)(2,1)S(1)}, bf16[96,768]{1,0:T(8,128)(2,1)S(1)}, bf16[96,768]{1,0:T(8,128)(2,1)S(1)}, bf16[96...) custom-call(bf16[128,512]{1,0:T(8,128)(2,1)S(1)} %get-tuple-element., ...), custom_call_target="tpu_custom_call" | custom-call | flops 603979776 | bytes 3145728 | tf_op jit(solution)/shard_map/mix/pallas_call | solution.py:318
  29.3 2.1 %collective-permute-start.9 = (bf16[96,768]{1,0:T(8,128)(2,1)S(1)}, bf16[96,768]{1,0:T(8,128)(2,1)S(1)}, u32[]{:S(2)}, u32[]{:S(2)}) collective-permute-start(bf16[96,768]{1,0:T(8,128)(2,1)S(1)} %get-tuple-element.94), channel_id=1, source_target_pairs={{0,1},{1,0},{2,3},{3,2},{4,5},{5,4},{6,7},{7,6},{8,9},{9,8},{10,11... | collective-permute-start | bytes 442376 | tf_op jit(solution)/shard_map/ppermute | solution.py:340
  31.4 2.5 %collective-permute-start.11 = (bf16[96,768]{1,0:T(8,128)(2,1)S(1)}, bf16[96,768]{1,0:T(8,128)(2,1)S(1)}, u32[]{:S(2)}, u32[]{:S(2)}) collective-permute-start(bf16[96,768]{1,0:T(8,128)(2,1)S(1)} %get-tuple-element.97), channel_id=1, source_target_pairs={{0,6},{1,7},{2,4},{3,5},{4,2},{5,3},{6,0},{7,1},{8,14},{9,15},{10,... | collective-permute-start | bytes 442376 | tf_op jit(solution)/shard_map/ppermute | solution.py:340
  34.0 1.5 %collective-permute-start.15 = (bf16[96,768]{1,0:T(8,128)(2,1)S(1)}, bf16[96,768]{1,0:T(8,128)(2,1)S(1)}, u32[]{:S(2)}, u32[]{:S(2)}) collective-permute-start(bf16[96,768]{1,0:T(8,128)(2,1)S(1)} %get-tuple-element.103), channel_id=1, source_target_pairs={{0,2},{1,3},{2,0},{3,1},{4,6},{5,7},{6,4},{7,5},{8,10},{9,11},{10,... | collective-permute-start | bytes 442376 | tf_op jit(solution)/shard_map/ppermute | solution.py:340
  35.5 1.3 %collective-permute-start.16 = (bf16[96,768]{1,0:T(8,128)(2,1)S(1)}, bf16[96,768]{1,0:T(8,128)(2,1)S(1)}, u32[]{:S(2)}, u32[]{:S(2)}) collective-permute-start(bf16[96,768]{1,0:T(8,128)(2,1)S(1)} %get-tuple-element.104), channel_id=1, source_target_pairs={{0,4},{1,5},{2,6},{3,7},{4,0},{5,1},{6,2},{7,3},{8,12},{9,13},{10,... | collective-permute-start | bytes 442376 | tf_op jit(solution)/shard_map/ppermute | solution.py:340
  37.6 1.8 %experts.4 = (bf16[96,768]{1,0:T(8,128)(2,1)S(1)}, bf16[96,768]{1,0:T(8,128)(2,1)S(1)}) custom-call(bf16[96,768]{1,0:T(8,128)(2,1)S(1)} %get-tuple-element.93.refs_0_, bf16[96,768]{1,0:T(8,128)(2,1)S(1)} %collective-permute-done.9.refs_1_, bf16[768,1536]{1,0:T(8,128)(2,1)S(1)} %bitcast.22, bf16[768,1536]{1,0:T(8,128)(2,1)S(1)} %bitcast.26, ...), custom_call_target="tpu_custom_call" | custom-call | flops 192 | bytes 192 | tf_op jit(solution)/shard_map/experts/pallas_call | solution.py:208
  41.6 1.8 %experts.5 = (bf16[96,768]{1,0:T(8,128)(2,1)S(1)}, bf16[96,768]{1,0:T(8,128)(2,1)S(1)}) custom-call(bf16[96,768]{1,0:T(8,128)(2,1)S(1)} %collective-permute-done.11.refs_0_, bf16[96,768]{1,0:T(8,128)(2,1)S(1)} %collective-permute-done.12.refs_1_, bf16[768,1536]{1,0:T(8,128)(2,1)S(1)} %bitcast.23, bf16[768,1536]{1,0:T(8,128)(2,1)S(1)} %bitcast.27, ...), custom_call_target="tpu_custom_call" | custom-call | flops 192 | bytes 192 | tf_op jit(solution)/shard_map/experts/pallas_call | solution.py:208
  44.5 2.3 %collective-permute-start.14 = (bf16[96,768]{1,0:T(8,128)(2,1)S(1)}, bf16[96,768]{1,0:T(8,128)(2,1)S(1)}, u32[]{:S(2)}, u32[]{:S(2)}) collective-permute-start(bf16[96,768]{1,0:T(8,128)(2,1)S(1)} %get-tuple-element.102), channel_id=1, source_target_pairs={{0,7},{1,6},{2,5},{3,4},{4,3},{5,2},{6,1},{7,0},{8,15},{9,14},{10,... | collective-permute-start | bytes 442376 | tf_op jit(solution)/shard_map/ppermute | solution.py:340
  48.0 1.8 %experts.6 = (bf16[96,768]{1,0:T(8,128)(2,1)S(1)}, bf16[96,768]{1,0:T(8,128)(2,1)S(1)}) custom-call(bf16[96,768]{1,0:T(8,128)(2,1)S(1)} %collective-permute-done.15.refs_0_, bf16[96,768]{1,0:T(8,128)(2,1)S(1)} %collective-permute-done.16.refs_1_, bf16[768,1536]{1,0:T(8,128)(2,1)S(1)} %bitcast.24, bf16[768,1536]{1,0:T(8,128)(2,1)S(1)} %bitcast.28, ...), custom_call_target="tpu_custom_call" | custom-call | flops 192 | bytes 192 | tf_op jit(solution)/shard_map/experts/pallas_call | solution.py:208
  50.0 1.4 %collective-permute-start.17 = (bf16[96,768]{1,0:T(8,128)(2,1)S(1)}, bf16[96,768]{1,0:T(8,128)(2,1)S(1)}, u32[]{:S(2)}, u32[]{:S(2)}) collective-permute-start(bf16[96,768]{1,0:T(8,128)(2,1)S(1)} %get-tuple-element.107), channel_id=1, source_target_pairs={{0,2},{1,3},{2,0},{3,1},{4,6},{5,7},{6,4},{7,5},{8,10},{9,11},{10,... | collective-permute-start | bytes 442376 | tf_op jit(solution)/shard_map/ppermute | solution.py:340
  51.4 1.8 %experts.7 = (bf16[96,768]{1,0:T(8,128)(2,1)S(1)}, bf16[96,768]{1,0:T(8,128)(2,1)S(1)}) custom-call(bf16[96,768]{1,0:T(8,128)(2,1)S(1)} %collective-permute-done.19.refs_0_, bf16[96,768]{1,0:T(8,128)(2,1)S(1)} %collective-permute-done.20.refs_1_, bf16[768,1536]{1,0:T(8,128)(2,1)S(1)} %bitcast.25, bf16[768,1536]{1,0:T(8,128)(2,1)S(1)} %bitcast.29, ...), custom_call_target="tpu_custom_call" | custom-call | flops 192 | bytes 192 | tf_op jit(solution)/shard_map/experts/pallas_call | solution.py:208
  55.2 2.9 %collective-permute-done.18.refs_5_ = bf16[96,768]{1,0:T(8,128)(2,1)S(1)} collective-permute-done((bf16[96,768]{1,0:T(8,128)(2,1)S(1)}, bf16[96,768]{1,0:T(8,128)(2,1)S(1)}, u32[]{:S(2)}, u32[]{:S(2)}) %collective-permute-start.18) | collective-permute-done | bytes 147488 | tf_op jit(solution)/shard_map/ppermute | solution.py:340
  58.1 2.6 %collective-permute-done.21.refs_6_ = bf16[96,768]{1,0:T(8,128)(2,1)S(1)} collective-permute-done((bf16[96,768]{1,0:T(8,128)(2,1)S(1)}, bf16[96,768]{1,0:T(8,128)(2,1)S(1)}, u32[]{:S(2)}, u32[]{:S(2)}) %collective-permute-start.21) | collective-permute-done | bytes 147488 | tf_op jit(solution)/shard_map/ppermute | solution.py:340
  61.3 1.8 %combine.1 = bf16[256,768]{1,0:T(8,128)(2,1)} custom-call(bf16[96,768]{1,0:T(8,128)(2,1)S(1)} %get-tuple-element.95.refs_0_, bf16[96,768]{1,0:T(8,128)(2,1)S(1)} %collective-permute-done.10.refs_1_, bf16[96,768]{1,0:T(8,128)(2,1)S(1)} %collective-permute-done.13.refs_2_, bf16[96,768]{1,0:T(8,128)(2,1)S(1)} %collective-permute-done.14.refs_3_, ...), custom_call_target="tpu_custom_call" | custom-call | flops 603979776 | bytes 1179648 | tf_op jit(solution)/shard_map/combine/pallas_call | solution.py:363
  (82 shorter events, 16.4 us)
Async XLA Ops:
  0.9 5.4 %collective-permute-start = (bf16[128,512]{1,0:T(8,128)(2,1)}, bf16[128,512]{1,0:T(8,128)(2,1)S(1)}, u32[]{:S(2)}, u32[]{:S(2)}) collective-permute-start(bf16[128,512]{1,0:T(8,128)(2,1)} %get-tuple-element.61), channel_id=1, source_target_pairs={{0,8},{1,9},{2,10},{3,11},{4,12},{5,13},{6,14},{7,15}} | collective-permute-start | bytes 393224 | tf_op jit(solution)/shard_map/ppermute | solution.py:278
  1.6 4.7 %collective-permute-start.3 = (bf16[128,512]{1,0:T(8,128)(2,1)}, bf16[128,512]{1,0:T(8,128)(2,1)S(1)}, u32[]{:S(2)}, u32[]{:S(2)}) collective-permute-start(bf16[128,512]{1,0:T(8,128)(2,1)} %get-tuple-element.80), channel_id=1, source_target_pairs={{0,8},{1,9},{2,10},{3,11},{4,12},{5,13},{6,14},{7,15}} | collective-permute-start | bytes 393224 | tf_op jit(solution)/shard_map/ppermute | solution.py:278
  2.3 6.5 %collective-permute-start.2 = (bf16[128,512]{1,0:T(8,128)(2,1)}, bf16[128,512]{1,0:T(8,128)(2,1)S(1)}, u32[]{:S(2)}, u32[]{:S(2)}) collective-permute-start(bf16[128,512]{1,0:T(8,128)(2,1)} %get-tuple-element.71), channel_id=1, source_target_pairs={{0,8},{1,9},{2,10},{3,11},{4,12},{5,13},{6,14},{7,15}} | collective-permute-start | bytes 393224 | tf_op jit(solution)/shard_map/ppermute | solution.py:278
  7.4 9.7 %collective-permute-start.4 = (bf16[128,512]{1,0:T(8,128)(2,1)S(1)}, bf16[128,512]{1,0:T(8,128)(2,1)S(1)}, u32[]{:S(2)}, u32[]{:S(2)}) collective-permute-start(bf16[128,512]{1,0:T(8,128)(2,1)S(1)} %fusion.4), channel_id=1, source_target_pairs={{8,16},{9,17},{10,18},{11,19},{12,20},{13,21},{14,22},{15,23}} | collective-permute-start | bytes 393224 | tf_op jit(solution)/shard_map/ppermute | solution.py:311
  8.7 18.2 %copy-start.4 = (bf16[1536,768]{1,0:T(8,128)(2,1)S(1)}, bf16[1536,768]{1,0:T(8,128)(2,1)}, u32[]{:S(2)}) copy-start(bf16[1536,768]{1,0:T(8,128)(2,1)} %refs_10_.1) | copy-start | bytes 7077892
  10.0 9.7 %collective-permute-start.5 = (bf16[128,512]{1,0:T(8,128)(2,1)S(1)}, bf16[128,512]{1,0:T(8,128)(2,1)S(1)}, u32[]{:S(2)}, u32[]{:S(2)}) collective-permute-start(bf16[128,512]{1,0:T(8,128)(2,1)S(1)} %get-tuple-element.73), channel_id=1, source_target_pairs={{8,16},{9,17},{10,18},{11,19},{12,20},{13,21},{14,22},{15,23}} | collective-permute-start | bytes 393224 | tf_op jit(solution)/shard_map/ppermute | solution.py:311
  11.3 11.2 %collective-permute-start.1 = (bf16[128,512]{1,0:T(8,128)(2,1)S(1)}, bf16[128,512]{1,0:T(8,128)(2,1)S(1)}, u32[]{:S(2)}, u32[]{:S(2)}) collective-permute-start(bf16[128,512]{1,0:T(8,128)(2,1)S(1)} %get-tuple-element.68), channel_id=1, source_target_pairs={{8,16},{9,17},{10,18},{11,19},{12,20},{13,21},{14,22},{15,23}} | collective-permute-start | bytes 393224 | tf_op jit(solution)/shard_map/ppermute | solution.py:311
  17.2 6.9 %collective-permute-start.7 = (bf16[128,512]{1,0:T(8,128)(2,1)S(1)}, bf16[128,512]{1,0:T(8,128)(2,1)S(1)}, u32[]{:S(2)}, u32[]{:S(2)}) collective-permute-start(bf16[128,512]{1,0:T(8,128)(2,1)S(1)} %get-tuple-element.88), channel_id=1, source_target_pairs={{16,24},{17,25},{18,26},{19,27},{20,28},{21,29},{22,30},{23,31}} | collective-permute-start | bytes 393224 | tf_op jit(solution)/shard_map/ppermute | solution.py:311
  19.8 4.4 %collective-permute-start.8 = (bf16[128,512]{1,0:T(8,128)(2,1)S(1)}, bf16[128,512]{1,0:T(8,128)(2,1)S(1)}, u32[]{:S(2)}, u32[]{:S(2)}) collective-permute-start(bf16[128,512]{1,0:T(8,128)(2,1)S(1)} %get-tuple-element.89), channel_id=1, source_target_pairs={{16,24},{17,25},{18,26},{19,27},{20,28},{21,29},{22,30},{23,31}} | collective-permute-start | bytes 393224 | tf_op jit(solution)/shard_map/ppermute | solution.py:311
  22.6 4.4 %collective-permute-start.6 = (bf16[128,512]{1,0:T(8,128)(2,1)S(1)}, bf16[128,512]{1,0:T(8,128)(2,1)S(1)}, u32[]{:S(2)}, u32[]{:S(2)}) collective-permute-start(bf16[128,512]{1,0:T(8,128)(2,1)S(1)} %get-tuple-element.87), channel_id=1, source_target_pairs={{16,24},{17,25},{18,26},{19,27},{20,28},{21,29},{22,30},{23,31}} | collective-permute-start | bytes 393224 | tf_op jit(solution)/shard_map/ppermute | solution.py:311
  29.3 7.4 %collective-permute-start.9 = (bf16[96,768]{1,0:T(8,128)(2,1)S(1)}, bf16[96,768]{1,0:T(8,128)(2,1)S(1)}, u32[]{:S(2)}, u32[]{:S(2)}) collective-permute-start(bf16[96,768]{1,0:T(8,128)(2,1)S(1)} %get-tuple-element.94), channel_id=1, source_target_pairs={{0,1},{1,0},{2,3},{3,2},{4,5},{5,4},{6,7},{7,6},{8,9},{9,8},{10,11... | collective-permute-start | bytes 442376 | tf_op jit(solution)/shard_map/ppermute | solution.py:340
  31.4 8.1 %collective-permute-start.11 = (bf16[96,768]{1,0:T(8,128)(2,1)S(1)}, bf16[96,768]{1,0:T(8,128)(2,1)S(1)}, u32[]{:S(2)}, u32[]{:S(2)}) collective-permute-start(bf16[96,768]{1,0:T(8,128)(2,1)S(1)} %get-tuple-element.97), channel_id=1, source_target_pairs={{0,6},{1,7},{2,4},{3,5},{4,2},{5,3},{6,0},{7,1},{8,14},{9,15},{10,... | collective-permute-start | bytes 442376 | tf_op jit(solution)/shard_map/ppermute | solution.py:340
  33.9 7.6 %collective-permute-start.12 = (bf16[96,768]{1,0:T(8,128)(2,1)S(1)}, bf16[96,768]{1,0:T(8,128)(2,1)S(1)}, u32[]{:S(2)}, u32[]{:S(2)}) collective-permute-start(bf16[96,768]{1,0:T(8,128)(2,1)S(1)} %get-tuple-element.98), channel_id=1, source_target_pairs={{0,7},{1,6},{2,5},{3,4},{4,3},{5,2},{6,1},{7,0},{8,15},{9,14},{10,... | collective-permute-start | bytes 442376 | tf_op jit(solution)/shard_map/ppermute | solution.py:340
  34.0 10.4 %collective-permute-start.15 = (bf16[96,768]{1,0:T(8,128)(2,1)S(1)}, bf16[96,768]{1,0:T(8,128)(2,1)S(1)}, u32[]{:S(2)}, u32[]{:S(2)}) collective-permute-start(bf16[96,768]{1,0:T(8,128)(2,1)S(1)} %get-tuple-element.103), channel_id=1, source_target_pairs={{0,2},{1,3},{2,0},{3,1},{4,6},{5,7},{6,4},{7,5},{8,10},{9,11},{10,... | collective-permute-start | bytes 442376 | tf_op jit(solution)/shard_map/ppermute | solution.py:340
  35.5 11.3 %collective-permute-start.16 = (bf16[96,768]{1,0:T(8,128)(2,1)S(1)}, bf16[96,768]{1,0:T(8,128)(2,1)S(1)}, u32[]{:S(2)}, u32[]{:S(2)}) collective-permute-start(bf16[96,768]{1,0:T(8,128)(2,1)S(1)} %get-tuple-element.104), channel_id=1, source_target_pairs={{0,4},{1,5},{2,6},{3,7},{4,0},{5,1},{6,2},{7,3},{8,12},{9,13},{10,... | collective-permute-start | bytes 442376 | tf_op jit(solution)/shard_map/ppermute | solution.py:340
  36.8 13.1 %collective-permute-start.19 = (bf16[96,768]{1,0:T(8,128)(2,1)S(1)}, bf16[96,768]{1,0:T(8,128)(2,1)S(1)}, u32[]{:S(2)}, u32[]{:S(2)}) collective-permute-start(bf16[96,768]{1,0:T(8,128)(2,1)S(1)} %get-tuple-element.109), channel_id=1, source_target_pairs={{0,3},{1,2},{2,1},{3,0},{4,7},{5,6},{6,5},{7,4},{8,11},{9,10},{10,... | collective-permute-start | bytes 442376 | tf_op jit(solution)/shard_map/ppermute | solution.py:340
  39.5 10.5 %collective-permute-start.20 = (bf16[96,768]{1,0:T(8,128)(2,1)S(1)}, bf16[96,768]{1,0:T(8,128)(2,1)S(1)}, u32[]{:S(2)}, u32[]{:S(2)}) collective-permute-start(bf16[96,768]{1,0:T(8,128)(2,1)S(1)} %get-tuple-element.110), channel_id=1, source_target_pairs={{0,5},{1,4},{2,7},{3,6},{4,1},{5,0},{6,3},{7,2},{8,13},{9,12},{10,... | collective-permute-start | bytes 442376 | tf_op jit(solution)/shard_map/ppermute | solution.py:340
  41.5 11.7 %collective-permute-start.10 = (bf16[96,768]{1,0:T(8,128)(2,1)S(1)}, bf16[96,768]{1,0:T(8,128)(2,1)S(1)}, u32[]{:S(2)}, u32[]{:S(2)}) collective-permute-start(bf16[96,768]{1,0:T(8,128)(2,1)S(1)} %get-tuple-element.96), channel_id=1, source_target_pairs={{0,1},{1,0},{2,3},{3,2},{4,5},{5,4},{6,7},{7,6},{8,9},{9,8},{10,11... | collective-permute-start | bytes 442376 | tf_op jit(solution)/shard_map/ppermute | solution.py:340
  44.5 9.8 %collective-permute-start.14 = (bf16[96,768]{1,0:T(8,128)(2,1)S(1)}, bf16[96,768]{1,0:T(8,128)(2,1)S(1)}, u32[]{:S(2)}, u32[]{:S(2)}) collective-permute-start(bf16[96,768]{1,0:T(8,128)(2,1)S(1)} %get-tuple-element.102), channel_id=1, source_target_pairs={{0,7},{1,6},{2,5},{3,4},{4,3},{5,2},{6,1},{7,0},{8,15},{9,14},{10,... | collective-permute-start | bytes 442376 | tf_op jit(solution)/shard_map/ppermute | solution.py:340
  46.8 8.5 %collective-permute-start.13 = (bf16[96,768]{1,0:T(8,128)(2,1)S(1)}, bf16[96,768]{1,0:T(8,128)(2,1)S(1)}, u32[]{:S(2)}, u32[]{:S(2)}) collective-permute-start(bf16[96,768]{1,0:T(8,128)(2,1)S(1)} %get-tuple-element.101), channel_id=1, source_target_pairs={{0,6},{1,7},{2,4},{3,5},{4,2},{5,3},{6,0},{7,1},{8,14},{9,15},{10,... | collective-permute-start | bytes 442376 | tf_op jit(solution)/shard_map/ppermute | solution.py:340
  49.9 8.2 %collective-permute-start.18 = (bf16[96,768]{1,0:T(8,128)(2,1)S(1)}, bf16[96,768]{1,0:T(8,128)(2,1)S(1)}, u32[]{:S(2)}, u32[]{:S(2)}) collective-permute-start(bf16[96,768]{1,0:T(8,128)(2,1)S(1)} %get-tuple-element.108), channel_id=1, source_target_pairs={{0,4},{1,5},{2,6},{3,7},{4,0},{5,1},{6,2},{7,3},{8,12},{9,13},{10,... | collective-permute-start | bytes 442376 | tf_op jit(solution)/shard_map/ppermute | solution.py:340
  50.0 8.1 %collective-permute-start.17 = (bf16[96,768]{1,0:T(8,128)(2,1)S(1)}, bf16[96,768]{1,0:T(8,128)(2,1)S(1)}, u32[]{:S(2)}, u32[]{:S(2)}) collective-permute-start(bf16[96,768]{1,0:T(8,128)(2,1)S(1)} %get-tuple-element.107), channel_id=1, source_target_pairs={{0,2},{1,3},{2,0},{3,1},{4,6},{5,7},{6,4},{7,5},{8,10},{9,11},{10,... | collective-permute-start | bytes 442376 | tf_op jit(solution)/shard_map/ppermute | solution.py:340
  53.2 7.5 %collective-permute-start.21 = (bf16[96,768]{1,0:T(8,128)(2,1)S(1)}, bf16[96,768]{1,0:T(8,128)(2,1)S(1)}, u32[]{:S(2)}, u32[]{:S(2)}) collective-permute-start(bf16[96,768]{1,0:T(8,128)(2,1)S(1)} %get-tuple-element.113), channel_id=1, source_target_pairs={{0,3},{1,2},{2,1},{3,0},{4,7},{5,6},{6,5},{7,4},{8,11},{9,10},{10,... | collective-permute-start | bytes 442376 | tf_op jit(solution)/shard_map/ppermute | solution.py:340
  54.2 7.0 %collective-permute-start.22 = (bf16[96,768]{1,0:T(8,128)(2,1)S(1)}, bf16[96,768]{1,0:T(8,128)(2,1)S(1)}, u32[]{:S(2)}, u32[]{:S(2)}) collective-permute-start(bf16[96,768]{1,0:T(8,128)(2,1)S(1)} %get-tuple-element.114), channel_id=1, source_target_pairs={{0,5},{1,4},{2,7},{3,6},{4,1},{5,0},{6,3},{7,2},{8,13},{9,12},{10,... | collective-permute-start | bytes 442376 | tf_op jit(solution)/shard_map/ppermute | solution.py:340
  (21 other events, 253.1 us)
